TPU v7x, 256 devices: a whole 4x4x8 slice. The times are simulated.
256 devices in a mesh: seq: 64 (over z, y, core), head: 4 (over x).
Axes of the slice: x: 4, y: 4, z: 8, core: 2. Of those that a mesh axis runs over, the one named last changes fastest.
Arguments:
- inputs: float32 [8192, 1024], P('seq', 'head'), may hold values from -6 to 6
- proj_weights: float32 [1024, 3, 512], P(None, None, 'head'), may hold values from -0.1875 to 0.1875
- out_grads: float32 [8192, 512], P('seq', 'head'), may hold values from -6 to 6
Outputs:
- grad_inputs: float32 [8192, 1024], P('seq', 'head')
- grad_weights: float32 [1024, 3, 512], P('seq', None, 'head')
All inputs are finite; a program needn't handle non-finite values.
Results may differ from a plain program's by a relative error of at most 0.0003.
Values sent between devices are 32-bit elements; how exact they have to be, the bound alone decides.
A program may use at most 128 MiB of HBM per device.

v0:
```python
import functools
import types

import jax
import jax.numpy as jnp
from jax import lax
from jax.experimental import pallas as pl
from jax.experimental.pallas import tpu as pltpu
from jax.sharding import PartitionSpec as P

MESH = pl.DeviceIdType.MESH
F32, BF16 = jnp.float32, jnp.bfloat16
E = 64
L = 128
T = 256
NX, NY, NZ = 4, 4, 8
LAST = 16
CHUNKS = ((128, 16, 8), (144, 24, 6))
VMEM = pl.BlockSpec(memory_space=pltpu.VMEM)
LIMIT = 56 * 2**20


def place():
    seq = lax.axis_index("seq")
    return lax.axis_index("head"), lax.rem(lax.div(seq, 2), NY), lax.div(seq, 2 * NY), lax.rem(seq, 2)


def device(x, y, z, c):
    return (z * (2 * NY) + y * 2 + c, x)


def remote(src, dst, send, recv, peer):
    return pltpu.make_async_remote_copy(
        src_ref=src, dst_ref=dst, send_sem=send, recv_sem=recv, device_id=peer, device_id_type=MESH
    )


def split(value):
    high = value.astype(BF16)
    return high, (value - high.astype(F32)).astype(BF16)


NN = (((1,), (0,)), ((), ()))
NT = (((1,), (1,)), ((), ()))
TN = (((0,), (0,)), ((), ()))


def dot(a, b, dims):
    return lax.dot_general(a, b, dims, preferred_element_type=F32)


def dot3(a, b, dims):
    return dot(a[0], b[0], dims) + (dot(a[0], b[1], dims) + dot(a[1], b[0], dims))


def lower():
    return lax.broadcasted_iota(jnp.int32, (1, L), 1) < E


def roll(value, shift):
    return pltpu.roll(value, shift, 1)


def shifted(double, block):
    return jnp.where(lower(), roll(double, E - 2 * block), roll(double, E - 1 - 2 * block))


def query_scale(block):
    distance = 2 * block + jnp.where(lower(), 0, 1)
    once = jnp.where(distance > 32, 0.0, 1.0 / E)
    return jnp.where((distance > 0) & (distance < 32), 2.0 / E, once)


def unshifted(term, block):
    low = lower()
    return roll(jnp.where(low, term, 0.0), 2 * block) + roll(jnp.where(low, 0.0, term), 2 * block + 1)


def folded(value):
    return value + roll(value, E)


def columns_of(double):
    high, low = split(double.T)
    return jnp.concatenate([high[:E], low[:E]], axis=0)


def state_block(columns, feats):
    product = dot(columns, feats, NN)
    product = product[:, :L] + product[:, L:]
    return product[:E] + product[E:]


def feature_pair(features):
    return jnp.concatenate(split(features), axis=1)


def rows_of(double):
    high, low = split(double)
    return jnp.concatenate([high[:, :E], low[:, :E], high[:, :E]], axis=1)


def apply_state(pair, parts):
    rows = jnp.concatenate(parts, axis=0)
    return dot(pair, jnp.concatenate([rows, rows], axis=1), NT)


def apply_rows(rows, parts):
    high, low = parts
    return dot(rows, jnp.concatenate([high, high, low], axis=0), NN)


class Chunk:
    def __init__(self, at, chunk, reverse, bufs, sems):
        self.rows, self.piece, self.owners = CHUNKS[chunk]
        self.at, self.reverse = at, reverse
        self.st, self.ry, self.py, self.tot, self.rz, self.pz, self.ez, self.oy, self.out = bufs
        s1, r1, s2, r2, s3, r3, s4, r4 = [sem.at[int(reverse), chunk] for sem in sems]
        y, z = at.y, at.z
        self.first = [None] + [
            remote(self.st.at[lax.rem(y + d, NY)], self.ry.at[d], s1.at[d], r1.at[d], at.py[d]) for d in range(1, NY)
        ]
        self.second, self.third = [None], [None]
        for d in range(1, NZ):
            target = lax.rem(z + d, NZ)
            self.second.append(
                remote(self.tot.at[self.part(target)], self.rz.at[d], s2.at[d], r2.at[d], at.pz[d])
            )
            self.third.append(remote(self.pz.at[target], self.ez.at[self.part(z)], s3.at[d], r3.at[d], at.pz[d]))
        self.fourth = [None] + [
            remote(self.oy.at[d], self.out.at[y], s4.at[d], r4.at[d], at.py[d]) for d in range(1, NY)
        ]

    def part(self, index):
        return pl.ds(pl.multiple_of(lax.min(index, self.owners - 1) * self.piece, 8), self.piece)

    def owner(self, index, act):
        if self.owners == NZ:
            act()
        else:
            pl.when(index < self.owners)(act)

    def ordered(self, n):
        return range(n - 1, -1, -1) if self.reverse else range(n)

    def totals(self):
        y, z = self.at.y, self.at.z
        for d in (1, 3, 2):
            self.first[d].wait_recv()
        running = jnp.zeros((self.rows, L), F32)
        for index in self.ordered(NY):
            self.py[index] = running
            running = running + self.ry[lax.rem(y + NY - index, NY)]
        self.tot[...] = running
        for d in (4, 3, 5, 2, 6, 1, 7):
            self.owner(lax.rem(z + d, NZ), self.second[d].start)

    def prefixes(self):
        z = self.at.z

        def act():
            self.rz[0] = self.tot[self.part(z)]
            for copy in self.second[1:]:
                copy.wait_recv()
            running = jnp.zeros((self.piece, L), F32)
            for index in self.ordered(NZ):
                self.pz[index] = running
                running = running + self.rz[lax.rem(z + NZ - index, NZ)]
            for d in (4, 3, 5, 2, 6, 1, 7):
                self.third[d].start()
            self.ez[self.part(z)] = self.pz[z]

        self.owner(z, act)

    def spread(self):
        y, z = self.at.y, self.at.z
        for d in range(1, NZ):
            self.owner(lax.rem(z + NZ - d, NZ), self.third[d].wait_recv)
        for d in (2, 1, 3):
            self.oy[d] = self.ez[...] + self.py[lax.rem(y + d, NY)]
            self.fourth[d].start()
        self.out[y] = self.ez[...] + self.py[y]

    def close(self):
        for d in range(1, NY):
            self.first[d].wait_send()
            self.fourth[d].wait_send()
        for d in range(1, NZ):
            self.owner(lax.rem(self.at.z + d, NZ), self.second[d].wait_send)

        def act():
            for copy in self.third[1:]:
                copy.wait_send()

        self.owner(self.at.z, act)


def fill(at, chunks, make, tail):
    for h, chunk in enumerate(chunks):
        if h == 1:
            rows = tail()
            for q in range(NY):
                chunk.st[q, 2 * E :] = rows[q * 16 : (q + 1) * 16]
        for d in (2, 1, 3, 0):
            q = lax.rem(at.y + d, NY)

            def step(i, carry):
                rows = pl.ds(pl.multiple_of(i * E, E), E)
                block = make(8 * h + 2 * q + i)
                if d == 0:
                    chunk.ry[0, rows] = block
                else:
                    chunk.st[q, rows] = block
                return carry

            lax.fori_loop(0, 2, step, 0, unroll=True)
            if d:
                chunk.first[d].start()
        if h == 1:
            chunk.ry[0, 2 * E :] = chunk.st[at.y, 2 * E :]


def tail_of(chunk):
    return jnp.concatenate([chunk.out[q, 2 * E :] for q in range(NY)], axis=0)


def over_blocks(at, chunks, step, carry, wait):
    for h, chunk in enumerate(chunks):
        for d in (0, 1, 3, 2):
            if wait and d:
                chunk.fourth[d].wait_recv()
            q = lax.rem(at.y + NY - d, NY)

            def inner(i, carry):
                rows = pl.ds(pl.multiple_of(i * E, E), E)
                return step(8 * h + 2 * q + i, split(chunk.out[q, rows]), carry)

            carry = lax.fori_loop(0, 2, inner, carry, unroll=True)
    return carry


def fused_kernel(names, *refs):
    r = types.SimpleNamespace(**dict(zip(names, refs)))
    x, y, z, c = place()
    at = types.SimpleNamespace(x=x, y=y, z=z, c=c)
    sibling = device(x, y, z, 1 - c)
    at.px = [None] + [device(lax.rem(x + d, NX), y, z, c) for d in range(1, NX)]
    at.py = [None] + [device(x, lax.rem(y + d, NY), z, c) for d in range(1, NY)]
    at.pz = [None] + [device(x, y, lax.rem(z + d, NZ), c) for d in range(1, NZ)]
    low = lower()

    load = pltpu.make_async_copy(r.w_in, r.w, r.wsem)
    load.start()
    barrier = pltpu.get_barrier_semaphore()
    peers = [sibling] + at.px[1:] + at.py[1:] + at.pz[1:]
    for peer in peers:
        pl.semaphore_signal(barrier, inc=1, device_id=peer, device_id_type=MESH)
    pl.semaphore_wait(barrier, len(peers))

    mine = pl.ds(pl.multiple_of(c * 128, 128), 128)
    over_x = [None] + [remote(r.x_in, r.xg.at[x, mine], r.xs.at[d], r.xr.at[d], at.px[d]) for d in range(1, NX)]
    for d in (2, 1, 3):
        over_x[d].start()
    own = remote(r.x_in, r.xg.at[x, mine], r.cs.at[0], r.cr.at[0], sibling)
    own.start()
    grads = remote(r.g_in, r.gg.at[mine], r.cs.at[1], r.cr.at[1], sibling)
    grads.start()
    r.xg[x, mine] = r.x_in[...]
    r.gg[mine] = r.g_in[...]
    load.wait()

    def split_weights(b, carry):
        rows = pl.ds(pl.multiple_of(b * 256, 256), 256)
        for i in range(3):
            r.wh[i, rows], r.wl[i, rows] = split(r.w[i, rows])
        return carry

    lax.fori_loop(0, NX, split_weights, 0)

    def project(b, sums):
        rows = pl.ds(pl.multiple_of(b * 256, 256), 256)
        r.xh[b], r.xl[b] = split(r.xg[b])
        feats = (r.xh[b], r.xl[b])
        return [sums[i] + dot3(feats, (r.wh[i, rows], r.wl[i, rows]), NN) for i in range(3)]

    own.wait_recv()
    sums = project(x, [jnp.zeros((T, L), F32) for _ in range(3)])
    forwards = [None] * NX
    order = (1, 3, 2)
    for d in order:
        over_x[d].wait_recv()
        source = lax.rem(x + NX - d, NX)
        forwards[d] = remote(r.xg.at[source, mine], r.xg.at[source, mine], r.fs.at[d], r.fr.at[d], sibling)
        forwards[d].start()
        forwards[d].wait_recv()
        sums = project(source, sums)

    def doubled(both):
        return jnp.where(low == (c == 0), both, roll(both, E))

    r.qq[...] = doubled(sums[0])
    r.kk[...] = doubled(sums[1])
    r.vv[...] = doubled(sums[2])

    scans = []
    for reverse in (False, True):
        bufs = [[buf[int(reverse)][h] for buf in r.bufs] for h in range(2)]
        scans.append([Chunk(at, h, reverse, bufs[h], r.sems) for h in range(2)])
    earlier, later = scans

    r.cols[...] = columns_of(r.vv[...])

    def key_block(block):
        kk = r.kk[...]
        return state_block(r.cols[...], feature_pair(kk * shifted(kk, block)))

    def key_tail():
        ks = split(r.kk[...])
        norm = dot3([k[:, :E] for k in ks], ks, TN)
        return jnp.where(low, key_block(LAST), norm)

    fill(at, earlier, key_block, key_tail)
    earlier[0].totals()
    earlier[1].totals()

    def query_feature(block, carry):
        qq = r.qq[...]
        r.feats[block] = feature_pair(qq * shifted(qq, block) * query_scale(block))
        return carry

    lax.fori_loop(0, LAST + 1, query_feature, 0)
    earlier[0].prefixes()
    earlier[1].prefixes()
    grads.wait_recv()
    causal = lax.broadcasted_iota(jnp.int32, (T, T), 0) >= lax.broadcasted_iota(jnp.int32, (T, T), 1)
    qs, ks, vs = [split(ref[...]) for ref in (r.qq, r.kk, r.vv)]
    r.dots[...] = dot3([v[:, :E] for v in qs], [v[:, :E] for v in ks], NT)
    weights = jnp.where(causal, r.dots[...] * r.dots[...] * (1.0 / E), 0.0)
    r.wgh[...], r.wgl[...] = split(weights)
    r.numer[...] = dot3((r.wgh[...], r.wgl[...]), vs, NN)
    r.denom[...] = jnp.broadcast_to(1.0 + jnp.sum(weights, axis=1, keepdims=True), (T, L))
    earlier[0].spread()
    earlier[1].spread()

    def forward(block, parts, total):
        return total + apply_state(r.feats[block], parts)

    total = over_blocks(at, earlier, forward, jnp.zeros((T, L), F32), True)
    tail = split(tail_of(earlier[1]))
    total = total + apply_state(r.feats[LAST], tail)
    qs = split(r.qq[...])
    normed = jnp.where(low, 0.0, dot3([v[:, :E] for v in qs], tail, NN))
    denom = r.denom[...] + jnp.sum(normed * r.qq[...], axis=1, keepdims=True) * (1.0 / E)
    inverse = 1.0 / denom
    grad_numer = doubled(r.gg[...]) * inverse
    grad_denom = -0.5 * jnp.sum(grad_numer * (r.numer[...] + folded(total)), axis=1, keepdims=True) * inverse
    r.gn[...] = grad_numer
    r.gd[...] = grad_denom

    r.cols[...] = columns_of(grad_numer)

    def query_block(block):
        return state_block(r.cols[...], r.feats[block])

    def query_tail():
        qq = r.qq[...]
        norm = dot3(split((qq * r.gd[...])[:, :E]), split(qq), TN) * (1.0 / E)
        return jnp.where(low, query_block(LAST), norm)

    fill(at, later, query_block, query_tail)
    later[0].totals()
    later[1].totals()

    r.rows[...] = rows_of(r.gn[...])

    def backward(block, parts, carry):
        one, two = carry
        qq = r.qq[...]
        grad = apply_rows(r.rows[...], parts) * query_scale(block)
        return one + grad * shifted(qq, block), two + unshifted(grad * qq, block)

    r.one[...] = normed * r.gd[...] * (2.0 / E)
    tail = split(tail_of(earlier[1]))
    carry = backward(LAST, tail, (r.one[...], jnp.zeros((T, L), F32)))
    one, two = over_blocks(at, earlier, backward, carry, False)
    r.one[...] = folded(one + two)
    later[0].prefixes()
    later[1].prefixes()
    qs, ks, vs, gs = [split(ref[...]) for ref in (r.qq, r.kk, r.vv, r.gn)]
    grad_scores = dot3([v[:, :E] for v in gs], [v[:, :E] for v in vs], NT) + r.gd[:, :1]
    grad_dots = split(jnp.where(causal, grad_scores, 0.0) * r.dots[...] * (2.0 / E))
    r.dq[...] = r.one[...] + dot3(grad_dots, ks, NN)
    r.dk[...] = dot3(grad_dots, qs, TN)
    r.dv[...] = dot3((r.wgh[...], r.wgl[...]), gs, TN)
    r.rows[...] = rows_of(r.vv[...])
    later[0].spread()
    later[1].spread()

    def keys(block, parts, carry, mask=None):
        total, one, two = carry
        kk = r.kk[...]
        shift = shifted(kk, block)
        if mask is not None:
            shift, kk = jnp.where(mask, shift, 0.0), jnp.where(mask, kk, 0.0)
        total = total + apply_state(feature_pair(kk * shift), parts)
        grad = apply_rows(r.rows[...], parts)
        return total, one + grad * shift, two + unshifted(grad * kk, block)

    zero = jnp.zeros((T, L), F32)
    carry = over_blocks(at, later, keys, (zero, zero, zero), True)
    tail = split(tail_of(later[1]))
    total, one, two = keys(LAST, tail, carry, low)
    ks = split(r.kk[...])
    normed = jnp.where(low, 0.0, dot3([v[:, :E] for v in ks], tail, NN))
    dv = r.dv[...] + folded(total)
    dk = r.dk[...] + folded(one + two + 2.0 * normed)
    dq = r.dq[...]
    for i, g in enumerate((dq, dk, dv)):
        r.gh[i], r.gl[i] = split(jnp.where(low == (c == 0), g, 0.0))
    r.ph[...], r.pl[...] = split(jnp.concatenate([jnp.where(low, dq, dk), dv], axis=1))

    first, second = [], []
    for h in range(2):
        for b in (2 * h, 2 * h + 1):
            grad = dot3((r.xh[b], r.xl[b]), (r.ph[...], r.pl[...]), TN)
            for i in range(8):
                rows = grad[i * 32 : (i + 1) * 32]
                at_y, at_z = i % NY, (b % 2) * 2 + i // NY
                r.dw[h, at_y, at_z, :32] = rows[:, :L]
                r.dw[h, at_y, at_z, 32:] = jnp.where(low, rows[:16, L:], rows[16:, L:])
        first.append(
            [None]
            + [
                remote(r.dw.at[h, lax.rem(y + d, NY)], r.wry.at[h, d], r.ws1.at[h, d], r.wr1.at[h, d], at.py[d])
                for d in range(1, NY)
            ]
        )
        for d in (2, 1, 3):
            first[h][d].start()

    across = [None] * NX
    for d in (2, 1, 3, 0):
        b = lax.rem(x + d, NX)
        rows = pl.ds(pl.multiple_of(b * 256, 256), 256)
        part = jnp.zeros((T, 256), F32)
        for i in range(3):
            part = part + dot3((r.gh[i], r.gl[i]), (r.wh[i, rows], r.wl[i, rows]), NT)
        r.dx[d, 0] = part[:128]
        r.dx[d, 1] = part[128:]
        across[d] = remote(r.dx.at[d, 1 - c], r.rc.at[d], r.as_.at[d], r.ar.at[d], sibling)
        across[d].start()

    out_x = [None] * NX
    for d in (2, 1, 3, 0):
        across[d].wait_recv()
        total = r.dx[d, c] + r.rc[d]
        if d:
            r.sx[d] = total
            out_x[d] = remote(r.sx.at[d], r.gx.at[d], r.os.at[d], r.or_.at[d], at.px[d])
            out_x[d].start()
        else:
            r.gx[0] = total

    for h in range(2):
        for d in (1, 3, 2):
            first[h][d].wait_recv()
        r.wty[h] = r.dw[h, y] + r.wry[h, 1] + r.wry[h, 2] + r.wry[h, 3]
    for d in range(1, NZ):
        target = lax.rem(z + d, NZ)
        second.append(
            remote(
                r.wty.at[lax.div(target, 4), lax.rem(target, 4)], r.wrz.at[d], r.ws2.at[d], r.wr2.at[d], at.pz[d]
            )
        )
    for d in (4, 3, 5, 2, 6, 1, 7):
        second[d - 1].start()
    total = r.wty[lax.div(z, 4), lax.rem(z, 4)]
    for d in (1, 7, 2, 6, 3, 5, 4):
        second[d - 1].wait_recv()
        total = total + r.wrz[d]
    r.gw[0] = total
    swap = remote(r.gw.at[0], r.gw.at[1], r.cs.at[2], r.cr.at[2], sibling)
    swap.start()
    for d in range(1, NX):
        out_x[d].wait()
    for copy in [own, grads] + over_x[1:] + forwards[1:] + first[0][1:] + first[1][1:] + second + across:
        copy.wait_send()
    for chunk in earlier + later:
        chunk.close()
    swap.wait()


def fused(inputs, weights, out_grads):
    dma = pltpu.SemaphoreType.DMA

    def vm(*shape, dtype=F32):
        return pltpu.VMEM(shape, dtype)

    scratch = dict(
        w=vm(3, 1024, L),
        wh=vm(3, 1024, L, dtype=BF16),
        wl=vm(3, 1024, L, dtype=BF16),
        xg=vm(NX, T, 256),
        xh=vm(NX, T, 256, dtype=BF16),
        xl=vm(NX, T, 256, dtype=BF16),
        gg=vm(T, L),
        qq=vm(T, L),
        kk=vm(T, L),
        vv=vm(T, L),
        cols=vm(L, T, dtype=BF16),
        rows=vm(T, 3 * E, dtype=BF16),
        feats=vm(LAST + 1, T, 2 * L, dtype=BF16),
        dots=vm(T, T),
        wgh=vm(T, T, dtype=BF16),
        wgl=vm(T, T, dtype=BF16),
        numer=vm(T, L),
        denom=vm(T, L),
        gn=vm(T, L),
        gd=vm(T, L),
        one=vm(T, L),
        dq=vm(T, L),
        dk=vm(T, L),
        dv=vm(T, L),
        gh=vm(3, T, L, dtype=BF16),
        gl=vm(3, T, L, dtype=BF16),
        ph=vm(T, 2 * L, dtype=BF16),
        pl=vm(T, 2 * L, dtype=BF16),
        dw=vm(2, NY, 4, 48, L),
        wry=vm(2, NY, 4, 48, L),
        wty=vm(2, 4, 48, L),
        wrz=vm(NZ, 48, L),
        dx=vm(NX, 2, 128, 256),
        rc=vm(NX, 128, 256),
        sx=vm(NX, 128, 256),
    )
    sems = dict(
        wsem=dma,
        xs=dma((NX,)),
        xr=dma((NX,)),
        fs=dma((NX,)),
        fr=dma((NX,)),
        cs=dma((3,)),
        cr=dma((3,)),
        ws1=dma((2, NY)),
        wr1=dma((2, NY)),
        ws2=dma((NZ,)),
        wr2=dma((NZ,)),
        as_=dma((NX,)),
        ar=dma((NX,)),
        os=dma((NX,)),
        or_=dma((NX,)),
    )
    bufs = [
        [
            [
                vm(NY, rows, L),
                vm(NY, rows, L),
                vm(NY, rows, L),
                vm(rows, L),
                vm(NZ, piece, L),
                vm(NZ, piece, L),
                vm(rows, L),
                vm(NY, rows, L),
                vm(NY, rows, L),
            ]
            for rows, piece, _ in CHUNKS
        ]
        for _ in range(2)
    ]
    scan_sems = [dma((2, 2, n)) for n in (NY, NY, NZ, NZ, NZ, NZ, NY, NY)]
    flat = list(scratch.values()) + list(sems.values()) + [b for s in bufs for h in s for b in h] + scan_sems
    names = ["x_in", "w_in", "g_in", "gx", "gw"] + list(scratch) + list(sems)

    def kernel(*refs):
        named, rest = refs[: len(names)], refs[len(names) :]
        held = [[[rest[(s * 2 + h) * 9 + i] for h in range(2)] for s in range(2)] for i in range(9)]
        fused_kernel(names + ["bufs", "sems"], *named, held, rest[36:])

    return pl.pallas_call(
        kernel,
        out_shape=(jax.ShapeDtypeStruct((NX, 128, 256), F32), jax.ShapeDtypeStruct((2, 48, L), F32)),
        in_specs=[VMEM, pl.BlockSpec(memory_space=pl.ANY), VMEM],
        out_specs=(VMEM, VMEM),
        scratch_shapes=flat,
        compiler_params=pltpu.CompilerParams(collective_id=0, has_side_effects=True, vmem_limit_bytes=LIMIT),
        name="fused",
    )(inputs, weights, out_grads)


def finish_kernel(gx, gw, dx, dw):
    c = lax.rem(lax.axis_index("seq"), 2)
    dx[...] = gx[0] + gx[1] + gx[2] + gx[3]
    low = lower()
    mine = pl.ds(pl.multiple_of(c * 16, 16), 16)

    def halves(rows):
        a, b = gw[0, rows], gw[1, rows]
        return jnp.where(c == 0, a, b), jnp.where(c == 0, b, a)

    zero, one = halves(mine)
    dw[:, 0, :] = jnp.where(low, zero, roll(one, E))
    dw[:, 1, :] = jnp.where(low, roll(zero, E), one)
    zero, one = halves(pl.ds(32, 16))
    dw[:, 2, :] = jnp.where(c == 0, jnp.where(low, zero, roll(one, E)), jnp.where(low, roll(zero, E), one))


def per_device(inputs, proj_weights, out_grads):
    gx, gw = fused(inputs, proj_weights.transpose(1, 0, 2), out_grads)
    return pl.pallas_call(
        finish_kernel,
        out_shape=(jax.ShapeDtypeStruct((128, 256), F32), jax.ShapeDtypeStruct((16, 3, L), F32)),
        in_specs=[VMEM, VMEM],
        out_specs=(VMEM, VMEM),
        name="finish",
    )(gx, gw)


def solution(mesh):
    return jax.shard_map(
        per_device,
        mesh=mesh,
        in_specs=(P("seq", "head"), P(None, None, "head"), P("seq", "head")),
        out_specs=(P("seq", "head"), P("seq", None, "head")),
        check_vma=False,
    )
```

profile of v0, /device:TPU:1, one launch (start us, length us, event | category | flops | bytes accessed | tf_op | source)
XLA Modules:
  0.0 94.9 jit_solution(18202822647386302084)
XLA Ops:
  0.6 91.1 %fused.1 = (f32[4,128,256]{2,1,0:T(8,128)}, f32[2,48,128]{2,1,0:T(8,128)}) custom-call(f32[128,256]{1,0:T(8,128)} %refs_0_.1, f32[3,1024,128]{2,1,0:T(8,128)} %bitcast.1, f32[128,128]{1,0:T(8,128)} %refs_2_.1), custom_call_target="tpu_custom_call" | custom-call | tf_op jit(solution)/shard_map/fused/pallas_call | solution.py:579
  91.7 1.8 %finish.1 = (f32[128,256]{1,0:T(8,128)}, f32[16,3,128]{2,1,0:T(4,128)}) custom-call(f32[4,128,256]{2,1,0:T(8,128)} %get-tuple-element.4.gx, f32[2,48,128]{2,1,0:T(8,128)} %get-tuple-element.5.gw), custom_call_target="tpu_custom_call" | custom-call | tf_op jit(solution)/shard_map/finish/pallas_call | solution.py:609
  93.5 1.4 %copy.5 = f32[16,3,128]{2,0,1:T(8,128)} copy(f32[16,3,128]{2,1,0:T(4,128)} %get-tuple-element.7) | data formatting | bytes 49152 | tf_op jit(solution)/shard_map/finish/pallas_call | solution.py:609
where the time goes:
time: 95.1 us; the launch traced here: 94.9 us
  Pallas kernels  92.9 us (98%)
  local copies, waits for them, and re-layouts  1.37 us (1%)
    pallas_call x1, Pallas kernels, fused(): pl.pallas_call(kernel, out_shape=(jax.ShapeDtypeStruct((NX, 128, 256), F3...  91.1 us

commit v1 on v0

--- a/solution.py
+++ b/solution.py
@@ -15,7 +15,8 @@
 T = 256
 NX, NY, NZ = 4, 4, 8
 LAST = 16
-CHUNKS = ((128, 16, 8), (144, 24, 6))
+CHUNKS = ((64, 8, 8), (64, 8, 8), (80, 16, 5), (64, 8, 8))
+WITH_LAST = 2
 VMEM = pl.BlockSpec(memory_space=pltpu.VMEM)
 LIMIT = 56 * 2**20
 
@@ -197,45 +198,31 @@
 
 def fill(at, chunks, make, tail):
     for h, chunk in enumerate(chunks):
-        if h == 1:
+        if h == WITH_LAST:
             rows = tail()
             for q in range(NY):
-                chunk.st[q, 2 * E :] = rows[q * 16 : (q + 1) * 16]
+                chunk.st[q, E:] = rows[q * 16 : (q + 1) * 16]
+            chunk.ry[0, E:] = chunk.st[at.y, E:]
         for d in (2, 1, 3, 0):
             q = lax.rem(at.y + d, NY)
-
-            def step(i, carry):
-                rows = pl.ds(pl.multiple_of(i * E, E), E)
-                block = make(8 * h + 2 * q + i)
-                if d == 0:
-                    chunk.ry[0, rows] = block
-                else:
-                    chunk.st[q, rows] = block
-                return carry
-
-            lax.fori_loop(0, 2, step, 0, unroll=True)
-            if d:
+            block = make(4 * h + q)
+            if d == 0:
+                chunk.ry[0, :E] = block
+            else:
+                chunk.st[q, :E] = block
                 chunk.first[d].start()
-        if h == 1:
-            chunk.ry[0, 2 * E :] = chunk.st[at.y, 2 * E :]
-
-
-def tail_of(chunk):
-    return jnp.concatenate([chunk.out[q, 2 * E :] for q in range(NY)], axis=0)
-
-
-def over_blocks(at, chunks, step, carry, wait):
-    for h, chunk in enumerate(chunks):
-        for d in (0, 1, 3, 2):
-            if wait and d:
-                chunk.fourth[d].wait_recv()
-            q = lax.rem(at.y + NY - d, NY)
-
-            def inner(i, carry):
-                rows = pl.ds(pl.multiple_of(i * E, E), E)
-                return step(8 * h + 2 * q + i, split(chunk.out[q, rows]), carry)
-
-            carry = lax.fori_loop(0, 2, inner, carry, unroll=True)
+
+
+def tail_of(chunks):
+    return split(jnp.concatenate([chunks[WITH_LAST].out[q, E:] for q in range(NY)], axis=0))
+
+
+def over_blocks(at, chunk, h, step, carry, wait):
+    for d in (0, 1, 3, 2):
+        if wait and d:
+            chunk.fourth[d].wait_recv()
+        q = lax.rem(at.y + NY - d, NY)
+        carry = step(4 * h + q, split(chunk.out[q, :E]), carry)
     return carry
 
 
@@ -255,16 +242,7 @@
     peers = [sibling] + at.px[1:] + at.py[1:] + at.pz[1:]
     for peer in peers:
         pl.semaphore_signal(barrier, inc=1, device_id=peer, device_id_type=MESH)
-    pl.semaphore_wait(barrier, len(peers))
-
     mine = pl.ds(pl.multiple_of(c * 128, 128), 128)
-    over_x = [None] + [remote(r.x_in, r.xg.at[x, mine], r.xs.at[d], r.xr.at[d], at.px[d]) for d in range(1, NX)]
-    for d in (2, 1, 3):
-        over_x[d].start()
-    own = remote(r.x_in, r.xg.at[x, mine], r.cs.at[0], r.cr.at[0], sibling)
-    own.start()
-    grads = remote(r.g_in, r.gg.at[mine], r.cs.at[1], r.cr.at[1], sibling)
-    grads.start()
     r.xg[x, mine] = r.x_in[...]
     r.gg[mine] = r.g_in[...]
     load.wait()
@@ -276,6 +254,21 @@
         return carry
 
     lax.fori_loop(0, NX, split_weights, 0)
+    pl.semaphore_wait(barrier, len(peers))
+
+    over_x = [[None] * NX, [None] * NX]
+    forwards = [[None] * NX, [None] * NX]
+    halves = [pl.ds(pl.multiple_of(c * 128 + 64 * k, 64), 64) for k in range(2)]
+    for k in range(2):
+        for d in (2, 1, 3):
+            over_x[k][d] = remote(
+                r.x_in.at[pl.ds(64 * k, 64)], r.xg.at[x, halves[k]], r.xs.at[k, d], r.xr.at[k, d], at.px[d]
+            )
+            over_x[k][d].start()
+    own = remote(r.x_in, r.xg.at[x, mine], r.cs.at[0], r.cr.at[0], sibling)
+    own.start()
+    grads = remote(r.g_in, r.gg.at[mine], r.cs.at[1], r.cr.at[1], sibling)
+    grads.start()
 
     def project(b, sums):
         rows = pl.ds(pl.multiple_of(b * 256, 256), 256)
@@ -285,15 +278,16 @@
 
     own.wait_recv()
     sums = project(x, [jnp.zeros((T, L), F32) for _ in range(3)])
-    forwards = [None] * NX
-    order = (1, 3, 2)
-    for d in order:
-        over_x[d].wait_recv()
-        source = lax.rem(x + NX - d, NX)
-        forwards[d] = remote(r.xg.at[source, mine], r.xg.at[source, mine], r.fs.at[d], r.fr.at[d], sibling)
-        forwards[d].start()
-        forwards[d].wait_recv()
-        sums = project(source, sums)
+    for k in range(2):
+        for d in (1, 3, 2):
+            over_x[k][d].wait_recv()
+            landed = r.xg.at[lax.rem(x + NX - d, NX), halves[k]]
+            forwards[k][d] = remote(landed, landed, r.fs.at[k, d], r.fr.at[k, d], sibling)
+            forwards[k][d].start()
+    for d in (1, 3, 2):
+        for k in range(2):
+            forwards[k][d].wait_recv()
+        sums = project(lax.rem(x + NX - d, NX), sums)
 
     def doubled(both):
         return jnp.where(low == (c == 0), both, roll(both, E))
@@ -304,8 +298,8 @@
 
     scans = []
     for reverse in (False, True):
-        bufs = [[buf[int(reverse)][h] for buf in r.bufs] for h in range(2)]
-        scans.append([Chunk(at, h, reverse, bufs[h], r.sems) for h in range(2)])
+        bufs = [[buf[int(reverse)][h] for buf in r.bufs] for h in range(len(CHUNKS))]
+        scans.append([Chunk(at, h, reverse, bufs[h], r.sems) for h in range(len(CHUNKS))])
     earlier, later = scans
 
     r.cols[...] = columns_of(r.vv[...])
@@ -320,17 +314,16 @@
         return jnp.where(low, key_block(LAST), norm)
 
     fill(at, earlier, key_block, key_tail)
-    earlier[0].totals()
-    earlier[1].totals()
 
     def query_feature(block, carry):
         qq = r.qq[...]
         r.feats[block] = feature_pair(qq * shifted(qq, block) * query_scale(block))
         return carry
 
-    lax.fori_loop(0, LAST + 1, query_feature, 0)
-    earlier[0].prefixes()
-    earlier[1].prefixes()
+    for h, chunk in enumerate(earlier):
+        chunk.totals()
+        lax.fori_loop(4 * h, 4 * h + 4, query_feature, 0)
+    query_feature(LAST, 0)
     grads.wait_recv()
     causal = lax.broadcasted_iota(jnp.int32, (T, T), 0) >= lax.broadcasted_iota(jnp.int32, (T, T), 1)
     qs, ks, vs = [split(ref[...]) for ref in (r.qq, r.kk, r.vv)]
@@ -339,14 +332,28 @@
     r.wgh[...], r.wgl[...] = split(weights)
     r.numer[...] = dot3((r.wgh[...], r.wgl[...]), vs, NN)
     r.denom[...] = jnp.broadcast_to(1.0 + jnp.sum(weights, axis=1, keepdims=True), (T, L))
-    earlier[0].spread()
-    earlier[1].spread()
+    for chunk in earlier:
+        chunk.prefixes()
+
+    def transposed(b, carry):
+        for to, value in ((r.xth, r.xh[b]), (r.xtl, r.xl[b])):
+            r.turned[...] = value.T
+            for i in range(8):
+                rows = pl.ds(pl.multiple_of(i * 32 + c * 16, 16), 16)
+                to[pl.ds(pl.multiple_of(b * 128 + i * 16, 16), 16)] = r.turned[rows]
+        return carry
+
+    lax.fori_loop(0, NX, transposed, 0)
+    for chunk in earlier:
+        chunk.spread()
 
     def forward(block, parts, total):
         return total + apply_state(r.feats[block], parts)
 
-    total = over_blocks(at, earlier, forward, jnp.zeros((T, L), F32), True)
-    tail = split(tail_of(earlier[1]))
+    total = jnp.zeros((T, L), F32)
+    for h, chunk in enumerate(earlier):
+        total = over_blocks(at, chunk, h, forward, total, True)
+    tail = tail_of(earlier)
     total = total + apply_state(r.feats[LAST], tail)
     qs = split(r.qq[...])
     normed = jnp.where(low, 0.0, dot3([v[:, :E] for v in qs], tail, NN))
@@ -368,8 +375,6 @@
         return jnp.where(low, query_block(LAST), norm)
 
     fill(at, later, query_block, query_tail)
-    later[0].totals()
-    later[1].totals()
 
     r.rows[...] = rows_of(r.gn[...])
 
@@ -380,21 +385,49 @@
         return one + grad * shifted(qq, block), two + unshifted(grad * qq, block)
 
     r.one[...] = normed * r.gd[...] * (2.0 / E)
-    tail = split(tail_of(earlier[1]))
-    carry = backward(LAST, tail, (r.one[...], jnp.zeros((T, L), F32)))
-    one, two = over_blocks(at, earlier, backward, carry, False)
-    r.one[...] = folded(one + two)
+    r.two[...] = jnp.zeros((T, L), F32)
+    for h, chunk in enumerate(later):
+        chunk.totals()
+        carry = (r.one[...], r.two[...])
+        if h == 0:
+            carry = backward(LAST, tail_of(earlier), carry)
+        r.one[...], r.two[...] = over_blocks(at, earlier[h], h, backward, carry, False)
+    qs, ks, vs, gs = [split(ref[...]) for ref in (r.qq, r.kk, r.vv, r.gn)]
+    grad_scores = dot3([v[:, :E] for v in gs], [v[:, :E] for v in vs], NT) + r.gd[:, :1]
+    r.gdh[...], r.gdl[...] = split(jnp.where(causal, grad_scores, 0.0) * r.dots[...] * (2.0 / E))
+    r.dq[...] = folded(r.one[...] + r.two[...]) + dot3((r.gdh[...], r.gdl[...]), ks, NN)
+    give_q = remote(r.dq, r.dqo, r.cs.at[2], r.cr.at[2], sibling)
+    give_q.start()
     later[0].prefixes()
     later[1].prefixes()
-    qs, ks, vs, gs = [split(ref[...]) for ref in (r.qq, r.kk, r.vv, r.gn)]
-    grad_scores = dot3([v[:, :E] for v in gs], [v[:, :E] for v in vs], NT) + r.gd[:, :1]
-    grad_dots = split(jnp.where(causal, grad_scores, 0.0) * r.dots[...] * (2.0 / E))
-    r.dq[...] = r.one[...] + dot3(grad_dots, ks, NN)
-    r.dk[...] = dot3(grad_dots, qs, TN)
+    give_q.wait_recv()
+    own_lanes = low == (c == 0)
+    r.gh[0], r.gl[0] = split(jnp.where(own_lanes, r.dq[...], r.dqo[...]))
+    for h in range(2):
+        rows = pl.ds(h * 256, 256)
+        grad = dot3((r.xth[rows], r.xtl[rows]), (r.gh[0], r.gl[0]), NN)
+        for i in range(16):
+            r.dwq[i % NY, 4 * h + i // NY] = grad[i * 16 : (i + 1) * 16]
+    q_y = [None] + [
+        remote(r.dwq.at[lax.rem(y + d, NY)], r.qry.at[d], r.qs1.at[d], r.qr1.at[d], at.py[d]) for d in range(1, NY)
+    ]
+    for d in (2, 1, 3):
+        q_y[d].start()
+    later[2].prefixes()
+    later[3].prefixes()
+    r.dk[...] = dot3((r.gdh[...], r.gdl[...]), qs, TN)
     r.dv[...] = dot3((r.wgh[...], r.wgl[...]), gs, TN)
     r.rows[...] = rows_of(r.vv[...])
-    later[0].spread()
-    later[1].spread()
+    for chunk in later:
+        chunk.spread()
+    for d in (1, 3, 2):
+        q_y[d].wait_recv()
+    r.qty[...] = r.dwq[y] + r.qry[1] + r.qry[2] + r.qry[3]
+    q_z = [None] + [
+        remote(r.qty.at[lax.rem(z + d, NZ)], r.qrz.at[d], r.qs2.at[d], r.qr2.at[d], at.pz[d]) for d in range(1, NZ)
+    ]
+    for d in (4, 3, 5, 2, 6, 1, 7):
+        q_z[d].start()
 
     def keys(block, parts, carry, mask=None):
         total, one, two = carry
@@ -407,27 +440,31 @@
         return total, one + grad * shift, two + unshifted(grad * kk, block)
 
     zero = jnp.zeros((T, L), F32)
-    carry = over_blocks(at, later, keys, (zero, zero, zero), True)
-    tail = split(tail_of(later[1]))
+    carry = (zero, zero, zero)
+    for h, chunk in enumerate(later):
+        carry = over_blocks(at, chunk, h, keys, carry, True)
+    tail = tail_of(later)
     total, one, two = keys(LAST, tail, carry, low)
     ks = split(r.kk[...])
     normed = jnp.where(low, 0.0, dot3([v[:, :E] for v in ks], tail, NN))
     dv = r.dv[...] + folded(total)
     dk = r.dk[...] + folded(one + two + 2.0 * normed)
-    dq = r.dq[...]
-    for i, g in enumerate((dq, dk, dv)):
-        r.gh[i], r.gl[i] = split(jnp.where(low == (c == 0), g, 0.0))
-    r.ph[...], r.pl[...] = split(jnp.concatenate([jnp.where(low, dq, dk), dv], axis=1))
-
-    first, second = [], []
+    r.kv[...] = jnp.where(low, dk, dv)
+    give_kv = remote(r.kv, r.kvo, r.cs.at[3], r.cr.at[3], sibling)
+    give_kv.start()
+    give_kv.wait_recv()
+    other = r.kvo[...]
+    turned = roll(other, E)
+    r.gh[1], r.gl[1] = split(jnp.where(own_lanes, dk, jnp.where(c == 0, turned, other)))
+    r.gh[2], r.gl[2] = split(jnp.where(own_lanes, dv, jnp.where(c == 0, other, turned)))
+
+    kv = [jnp.concatenate([g[1], g[2]], axis=1) for g in (r.gh, r.gl)]
+    first = []
     for h in range(2):
-        for b in (2 * h, 2 * h + 1):
-            grad = dot3((r.xh[b], r.xl[b]), (r.ph[...], r.pl[...]), TN)
-            for i in range(8):
-                rows = grad[i * 32 : (i + 1) * 32]
-                at_y, at_z = i % NY, (b % 2) * 2 + i // NY
-                r.dw[h, at_y, at_z, :32] = rows[:, :L]
-                r.dw[h, at_y, at_z, 32:] = jnp.where(low, rows[:16, L:], rows[16:, L:])
+        rows = pl.ds(h * 256, 256)
+        grad = dot3((r.xth[rows], r.xtl[rows]), kv, NN)
+        for i in range(16):
+            r.dw[h, i % NY, i // NY] = grad[i * 16 : (i + 1) * 16]
         first.append(
             [None]
             + [
@@ -438,56 +475,53 @@
         for d in (2, 1, 3):
             first[h][d].start()
 
-    across = [None] * NX
-    for d in (2, 1, 3, 0):
-        b = lax.rem(x + d, NX)
-        rows = pl.ds(pl.multiple_of(b * 256, 256), 256)
-        part = jnp.zeros((T, 256), F32)
-        for i in range(3):
-            part = part + dot3((r.gh[i], r.gl[i]), (r.wh[i, rows], r.wl[i, rows]), NT)
-        r.dx[d, 0] = part[:128]
-        r.dx[d, 1] = part[128:]
-        across[d] = remote(r.dx.at[d, 1 - c], r.rc.at[d], r.as_.at[d], r.ar.at[d], sibling)
-        across[d].start()
-
     out_x = [None] * NX
     for d in (2, 1, 3, 0):
-        across[d].wait_recv()
-        total = r.dx[d, c] + r.rc[d]
+        rows = pl.ds(pl.multiple_of(lax.rem(x + d, NX) * 256, 256), 256)
+        part = jnp.zeros((128, 256), F32)
+        for i in range(3):
+            part = part + dot3((r.gh[i, mine], r.gl[i, mine]), (r.wh[i, rows], r.wl[i, rows]), NT)
+        r.sx[d] = part
         if d:
-            r.sx[d] = total
-            out_x[d] = remote(r.sx.at[d], r.gx.at[d], r.os.at[d], r.or_.at[d], at.px[d])
+            out_x[d] = remote(r.sx.at[d], r.rx.at[d], r.os.at[d], r.or_.at[d], at.px[d])
             out_x[d].start()
-        else:
-            r.gx[0] = total
 
     for h in range(2):
         for d in (1, 3, 2):
             first[h][d].wait_recv()
         r.wty[h] = r.dw[h, y] + r.wry[h, 1] + r.wry[h, 2] + r.wry[h, 3]
+        for j in (0, 3, 1, 2):
+            target = 4 * h + j
+            d = lax.rem(target - z + NZ, NZ)
+            copy = remote(r.wty.at[h, j], r.wrz.at[d], r.ws2.at[d], r.wr2.at[d], device(x, y, target, c))
+            pl.when(target != z)(copy.start)
+    for d in (1, 3, 2):
+        out_x[d].wait_recv()
+    r.gx[...] = r.sx[0] + r.rx[1] + r.rx[2] + r.rx[3]
+    total = r.qty[z]
     for d in range(1, NZ):
-        target = lax.rem(z + d, NZ)
-        second.append(
-            remote(
-                r.wty.at[lax.div(target, 4), lax.rem(target, 4)], r.wrz.at[d], r.ws2.at[d], r.wr2.at[d], at.pz[d]
-            )
+        q_z[d].wait_recv()
+        total = total + r.qrz[d]
+    r.gw[0] = total
+    total = r.wty[lax.div(z, 4), lax.rem(z, 4)]
+    second = [
+        remote(
+            r.wty.at[lax.div(lax.rem(z + d, NZ), 4), lax.rem(z + d, 4)], r.wrz.at[d], r.ws2.at[d], r.wr2.at[d], at.pz[d]
         )
-    for d in (4, 3, 5, 2, 6, 1, 7):
-        second[d - 1].start()
-    total = r.wty[lax.div(z, 4), lax.rem(z, 4)]
+        for d in range(1, NZ)
+    ]
     for d in (1, 7, 2, 6, 3, 5, 4):
         second[d - 1].wait_recv()
         total = total + r.wrz[d]
-    r.gw[0] = total
-    swap = remote(r.gw.at[0], r.gw.at[1], r.cs.at[2], r.cr.at[2], sibling)
-    swap.start()
-    for d in range(1, NX):
-        out_x[d].wait()
-    for copy in [own, grads] + over_x[1:] + forwards[1:] + first[0][1:] + first[1][1:] + second + across:
+    r.gw[1] = total[:, :L]
+    r.gw[2] = total[:, L:]
+    sent = [own, grads, give_q, give_kv] + second
+    for group in over_x + forwards + first + [out_x, q_y, q_z]:
+        sent += group[1:]
+    for copy in sent:
         copy.wait_send()
     for chunk in earlier + later:
         chunk.close()
-    swap.wait()
 
 
 def fused(inputs, weights, out_grads):
@@ -521,32 +555,44 @@
         dq=vm(T, L),
         dk=vm(T, L),
         dv=vm(T, L),
+        two=vm(T, L),
+        gdh=vm(T, T, dtype=BF16),
+        gdl=vm(T, T, dtype=BF16),
+        dqo=vm(T, L),
+        kv=vm(T, L),
+        kvo=vm(T, L),
         gh=vm(3, T, L, dtype=BF16),
         gl=vm(3, T, L, dtype=BF16),
-        ph=vm(T, 2 * L, dtype=BF16),
-        pl=vm(T, 2 * L, dtype=BF16),
-        dw=vm(2, NY, 4, 48, L),
-        wry=vm(2, NY, 4, 48, L),
-        wty=vm(2, 4, 48, L),
-        wrz=vm(NZ, 48, L),
-        dx=vm(NX, 2, 128, 256),
-        rc=vm(NX, 128, 256),
+        turned=vm(256, T, dtype=BF16),
+        xth=vm(512, T, dtype=BF16),
+        xtl=vm(512, T, dtype=BF16),
+        dwq=vm(NY, NZ, 16, L),
+        qry=vm(NY, NZ, 16, L),
+        qty=vm(NZ, 16, L),
+        qrz=vm(NZ, 16, L),
+        dw=vm(2, NY, 4, 16, 2 * L),
+        wry=vm(2, NY, 4, 16, 2 * L),
+        wty=vm(2, 4, 16, 2 * L),
+        wrz=vm(NZ, 16, 2 * L),
         sx=vm(NX, 128, 256),
+        rx=vm(NX, 128, 256),
     )
     sems = dict(
         wsem=dma,
-        xs=dma((NX,)),
-        xr=dma((NX,)),
-        fs=dma((NX,)),
-        fr=dma((NX,)),
-        cs=dma((3,)),
-        cr=dma((3,)),
+        xs=dma((2, NX)),
+        xr=dma((2, NX)),
+        fs=dma((2, NX)),
+        fr=dma((2, NX)),
+        cs=dma((4,)),
+        cr=dma((4,)),
+        qs1=dma((NY,)),
+        qr1=dma((NY,)),
+        qs2=dma((NZ,)),
+        qr2=dma((NZ,)),
         ws1=dma((2, NY)),
         wr1=dma((2, NY)),
         ws2=dma((NZ,)),
         wr2=dma((NZ,)),
-        as_=dma((NX,)),
-        ar=dma((NX,)),
         os=dma((NX,)),
         or_=dma((NX,)),
     )
@@ -567,18 +613,19 @@
         ]
         for _ in range(2)
     ]
-    scan_sems = [dma((2, 2, n)) for n in (NY, NY, NZ, NZ, NZ, NZ, NY, NY)]
+    scan_sems = [dma((2, len(CHUNKS), n)) for n in (NY, NY, NZ, NZ, NZ, NZ, NY, NY)]
     flat = list(scratch.values()) + list(sems.values()) + [b for s in bufs for h in s for b in h] + scan_sems
     names = ["x_in", "w_in", "g_in", "gx", "gw"] + list(scratch) + list(sems)
 
     def kernel(*refs):
         named, rest = refs[: len(names)], refs[len(names) :]
-        held = [[[rest[(s * 2 + h) * 9 + i] for h in range(2)] for s in range(2)] for i in range(9)]
-        fused_kernel(names + ["bufs", "sems"], *named, held, rest[36:])
+        count = len(CHUNKS)
+        held = [[[rest[(s * count + h) * 9 + i] for h in range(count)] for s in range(2)] for i in range(9)]
+        fused_kernel(names + ["bufs", "sems"], *named, held, rest[18 * count :])
 
     return pl.pallas_call(
         kernel,
-        out_shape=(jax.ShapeDtypeStruct((NX, 128, 256), F32), jax.ShapeDtypeStruct((2, 48, L), F32)),
+        out_shape=(jax.ShapeDtypeStruct((128, 256), F32), jax.ShapeDtypeStruct((3, 16, L), F32)),
         in_specs=[VMEM, pl.BlockSpec(memory_space=pl.ANY), VMEM],
         out_specs=(VMEM, VMEM),
         scratch_shapes=flat,
@@ -588,31 +635,20 @@
 
 
 def finish_kernel(gx, gw, dx, dw):
-    c = lax.rem(lax.axis_index("seq"), 2)
-    dx[...] = gx[0] + gx[1] + gx[2] + gx[3]
-    low = lower()
-    mine = pl.ds(pl.multiple_of(c * 16, 16), 16)
-
-    def halves(rows):
-        a, b = gw[0, rows], gw[1, rows]
-        return jnp.where(c == 0, a, b), jnp.where(c == 0, b, a)
-
-    zero, one = halves(mine)
-    dw[:, 0, :] = jnp.where(low, zero, roll(one, E))
-    dw[:, 1, :] = jnp.where(low, roll(zero, E), one)
-    zero, one = halves(pl.ds(32, 16))
-    dw[:, 2, :] = jnp.where(c == 0, jnp.where(low, zero, roll(one, E)), jnp.where(low, roll(zero, E), one))
+    dx[...] = gx[...]
+    dw[...] = gw[...]
 
 
 def per_device(inputs, proj_weights, out_grads):
     gx, gw = fused(inputs, proj_weights.transpose(1, 0, 2), out_grads)
-    return pl.pallas_call(
+    dx, dw = pl.pallas_call(
         finish_kernel,
-        out_shape=(jax.ShapeDtypeStruct((128, 256), F32), jax.ShapeDtypeStruct((16, 3, L), F32)),
+        out_shape=(jax.ShapeDtypeStruct((128, 256), F32), jax.ShapeDtypeStruct((3, 16, L), F32)),
         in_specs=[VMEM, VMEM],
         out_specs=(VMEM, VMEM),
         name="finish",
     )(gx, gw)
+    return dx, dw.transpose(1, 0, 2)
 
 
 def solution(mesh):

time: 95.1 us -> 86.8 us (0.913)
  Pallas kernels: 92.9 us -> 86 us
  local copies, waits for them, and re-layouts: 1.37 us -> 0 us
    pallas_call x1, Pallas kernels: 91.1 us -> 84.4 us  [fused(): pl.pallas_call(kernel, out_shape=(jax.ShapeDtypeStruct((128, 256), F32),...]
    pallas_call x1 -> x0, local copies, waits for them, and re-layouts: 1.37 us -> none  [per_device(): pl.pallas_call(finish_kernel, out_shape=(jax.ShapeDtypeStruct((128, 256),...]
where the time goes in v1:
time: 86.8 us; the launch traced here: 86.6 us
  Pallas kernels  86 us (99%)
    pallas_call x1, Pallas kernels, fused(): pl.pallas_call(kernel, out_shape=(jax.ShapeDtypeStruct((128, 256), F32),...  84.4 us

profile of v1, /device:TPU:1, one launch (start us, length us, event | category | flops | bytes accessed | tf_op | source)
XLA Modules:
  0.0 86.6 jit_solution(6159871438086675591)
XLA Ops:
  0.6 84.4 %fused.1 = (f32[128,256]{1,0:T(8,128)}, f32[3,16,128]{2,1,0:T(8,128)}) custom-call(f32[128,256]{1,0:T(8,128)} %refs_0_.1, f32[3,1024,128]{2,1,0:T(8,128)} %bitcast.2, f32[128,128]{1,0:T(8,128)} %refs_2_.1), custom_call_target="tpu_custom_call" | custom-call | tf_op jit(solution)/shard_map/fused/pallas_call | solution.py:626
  85.1 1.6 %finish.1 = (f32[128,256]{1,0:T(8,128)}, f32[3,16,128]{2,1,0:T(8,128)}) custom-call(f32[128,256]{1,0:T(8,128)} %get-tuple-element.6.gx, f32[3,16,128]{2,1,0:T(8,128)} %get-tuple-element.7.gw), custom_call_target="tpu_custom_call" | custom-call | tf_op jit(solution)/shard_map/finish/pallas_call | solution.py:644

commit v2 on v1

--- a/solution.py
+++ b/solution.py
@@ -36,6 +36,10 @@
     )
 
 
+def settle(ref, send, recv, peer):
+    return remote(ref, ref, send, recv, peer)
+
+
 def split(value):
     high = value.astype(BF16)
     return high, (value - high.astype(F32)).astype(BF16)
@@ -116,38 +120,42 @@
         self.rows, self.piece, self.owners = CHUNKS[chunk]
         self.at, self.reverse = at, reverse
         self.st, self.ry, self.py, self.tot, self.rz, self.pz, self.ez, self.oy, self.out = bufs
-        s1, r1, s2, r2, s3, r3, s4, r4 = [sem.at[int(reverse), chunk] for sem in sems]
+        send, recv = [[sem.at[int(reverse), chunk, stage] for stage in range(4)] for sem in sems]
         y, z = at.y, at.z
         self.first = [None] + [
-            remote(self.st.at[lax.rem(y + d, NY)], self.ry.at[d], s1.at[d], r1.at[d], at.py[d]) for d in range(1, NY)
+            remote(self.st.at[lax.rem(y + d, NY)], self.ry.at[d], send[0], recv[0], at.py[d]) for d in range(1, NY)
         ]
         self.second, self.third = [None], [None]
         for d in range(1, NZ):
             target = lax.rem(z + d, NZ)
-            self.second.append(
-                remote(self.tot.at[self.part(target)], self.rz.at[d], s2.at[d], r2.at[d], at.pz[d])
-            )
-            self.third.append(remote(self.pz.at[target], self.ez.at[self.part(z)], s3.at[d], r3.at[d], at.pz[d]))
+            self.second.append(remote(self.tot.at[self.part(target)], self.rz.at[d], send[1], recv[1], at.pz[d]))
+            self.third.append(remote(self.pz.at[target], self.ez.at[self.part(z)], send[2], recv[2], at.pz[d]))
         self.fourth = [None] + [
-            remote(self.oy.at[d], self.out.at[y], s4.at[d], r4.at[d], at.py[d]) for d in range(1, NY)
+            remote(self.oy.at[d], self.out.at[y], send[3], recv[3], at.py[d]) for d in range(1, NY)
         ]
+        self.send, self.recv = send, recv
+
+    def all_of(self, stage, pieces=NZ - 1):
+        ref = self.ry.at[pl.ds(1, NY - 1)] if stage in (0, 3) else self.rz.at[pl.ds(0, pieces)]
+        return settle(ref, self.send[stage], self.recv[stage], self.at.py[1])
 
     def part(self, index):
         return pl.ds(pl.multiple_of(lax.min(index, self.owners - 1) * self.piece, 8), self.piece)
 
-    def owner(self, index, act):
+    def owner(self, index, act, otherwise=None):
         if self.owners == NZ:
             act()
         else:
             pl.when(index < self.owners)(act)
+            if otherwise is not None:
+                pl.when(index >= self.owners)(otherwise)
 
     def ordered(self, n):
         return range(n - 1, -1, -1) if self.reverse else range(n)
 
     def totals(self):
         y, z = self.at.y, self.at.z
-        for d in (1, 3, 2):
-            self.first[d].wait_recv()
+        self.all_of(0).wait_recv()
         running = jnp.zeros((self.rows, L), F32)
         for index in self.ordered(NY):
             self.py[index] = running
@@ -161,8 +169,7 @@
 
         def act():
             self.rz[0] = self.tot[self.part(z)]
-            for copy in self.second[1:]:
-                copy.wait_recv()
+            self.all_of(1).wait_recv()
             running = jnp.zeros((self.piece, L), F32)
             for index in self.ordered(NZ):
                 self.pz[index] = running
@@ -175,42 +182,81 @@
 
     def spread(self):
         y, z = self.at.y, self.at.z
-        for d in range(1, NZ):
-            self.owner(lax.rem(z + NZ - d, NZ), self.third[d].wait_recv)
+        self.owner(
+            z,
+            lambda: self.all_of(2, self.owners - 1).wait_recv(),
+            lambda: self.all_of(2, self.owners).wait_recv(),
+        )
         for d in (2, 1, 3):
             self.oy[d] = self.ez[...] + self.py[lax.rem(y + d, NY)]
             self.fourth[d].start()
         self.out[y] = self.ez[...] + self.py[y]
 
     def close(self):
+        self.all_of(0).wait_send()
+        self.owner(
+            self.at.z,
+            lambda: self.all_of(1, self.owners - 1).wait_send(),
+            lambda: self.all_of(1, self.owners).wait_send(),
+        )
+        self.owner(self.at.z, lambda: self.all_of(2).wait_send())
+        self.all_of(3).wait_send()
+
+
+class Norms:
+    def __init__(self, at, reverse, bufs, sems):
+        self.at, self.reverse = at, reverse
+        self.own, self.ry, self.tot, self.rz = bufs
+        send, recv = [[sem.at[int(reverse), stage] for stage in range(2)] for sem in sems]
+        self.first = [remote(self.own, self.ry.at[d], send[0], recv[0], at.py[d]) for d in (2, 1, 3)]
+        self.second = [remote(self.tot, self.rz.at[d], send[1], recv[1], at.pz[d]) for d in (4, 3, 5, 2, 6, 1, 7)]
+        self.all_first = settle(self.ry.at[pl.ds(1, NY - 1)], send[0], recv[0], at.py[1])
+        self.all_second = settle(self.rz.at[pl.ds(1, NZ - 1)], send[1], recv[1], at.pz[1])
+
+    def counts(self, d, index):
+        return d > index if self.reverse else d <= index
+
+    def start(self, matrix):
+        self.own[...] = jnp.where(lower(), matrix[:32], matrix[32:])
+        for copy in self.first:
+            copy.start()
+
+    def relay(self):
+        self.all_first.wait_recv()
+        self.tot[...] = self.own[...] + self.ry[1] + self.ry[2] + self.ry[3]
+        for copy in self.second:
+            copy.start()
+
+    def result(self):
+        self.all_second.wait_recv()
+        total = jnp.zeros((32, L), F32)
+        for d in range(1, NZ):
+            total = total + jnp.where(self.counts(d, self.at.z), self.rz[d], 0.0)
         for d in range(1, NY):
-            self.first[d].wait_send()
-            self.fourth[d].wait_send()
-        for d in range(1, NZ):
-            self.owner(lax.rem(self.at.z + d, NZ), self.second[d].wait_send)
-
-        def act():
-            for copy in self.third[1:]:
-                copy.wait_send()
-
-        self.owner(self.at.z, act)
-
-
-def fill(at, chunks, make, tail):
-    for h, chunk in enumerate(chunks):
-        if h == WITH_LAST:
-            rows = tail()
-            for q in range(NY):
-                chunk.st[q, E:] = rows[q * 16 : (q + 1) * 16]
-            chunk.ry[0, E:] = chunk.st[at.y, E:]
-        for d in (2, 1, 3, 0):
-            q = lax.rem(at.y + d, NY)
-            block = make(4 * h + q)
-            if d == 0:
-                chunk.ry[0, :E] = block
-            else:
-                chunk.st[q, :E] = block
-                chunk.first[d].start()
+            total = total + jnp.where(self.counts(d, self.at.y), self.ry[d], 0.0)
+        turned = roll(total, E)
+        low = lower()
+        return split(jnp.concatenate([jnp.where(low, total, turned), jnp.where(low, turned, total)], axis=0))
+
+    def close(self):
+        self.all_first.wait_send()
+        self.all_second.wait_send()
+
+
+def fill(at, chunk, h, make):
+    if h == WITH_LAST:
+        rows = make(LAST)
+        for q in range(NY):
+            chunk.st[q, E:] = rows[q * 16 : (q + 1) * 16]
+        chunk.ry[0, E:] = chunk.st[at.y, E:]
+    for d in (2, 1, 3, 0):
+        q = lax.rem(at.y + d, NY)
+        block = make(4 * h + q)
+        if d == 0:
+            chunk.ry[0, :E] = block
+        else:
+            chunk.st[q, :E] = block
+            chunk.first[d].start()
 
 
 def tail_of(chunks):
@@ -218,9 +264,9 @@
 
 
 def over_blocks(at, chunk, h, step, carry, wait):
-    for d in (0, 1, 3, 2):
-        if wait and d:
-            chunk.fourth[d].wait_recv()
+    for d in range(NY):
+        if wait and d == 1:
+            chunk.all_of(3).wait_recv()
         q = lax.rem(at.y + NY - d, NY)
         carry = step(4 * h + q, split(chunk.out[q, :E]), carry)
     return carry
@@ -262,7 +308,7 @@
     for k in range(2):
         for d in (2, 1, 3):
             over_x[k][d] = remote(
-                r.x_in.at[pl.ds(64 * k, 64)], r.xg.at[x, halves[k]], r.xs.at[k, d], r.xr.at[k, d], at.px[d]
+                r.x_in.at[pl.ds(64 * k, 64)], r.xg.at[x, halves[k]], r.xs, r.xr.at[k, d], at.px[d]
             )
             over_x[k][d].start()
     own = remote(r.x_in, r.xg.at[x, mine], r.cs.at[0], r.cr.at[0], sibling)
@@ -282,7 +328,7 @@
         for d in (1, 3, 2):
             over_x[k][d].wait_recv()
             landed = r.xg.at[lax.rem(x + NX - d, NX), halves[k]]
-            forwards[k][d] = remote(landed, landed, r.fs.at[k, d], r.fr.at[k, d], sibling)
+            forwards[k][d] = remote(landed, landed, r.fs, r.fr.at[k, d], sibling)
             forwards[k][d].start()
     for d in (1, 3, 2):
         for k in range(2):
@@ -302,18 +348,20 @@
         scans.append([Chunk(at, h, reverse, bufs[h], r.sems) for h in range(len(CHUNKS))])
     earlier, later = scans
 
+    norms, adjoint_norms = [Norms(at, v, r.small[int(v)], r.small_sems) for v in (False, True)]
+    ks = split(r.kk[...])
+    norms.start(dot3([v[:, :E] for v in ks], ks, TN))
+
     r.cols[...] = columns_of(r.vv[...])
 
     def key_block(block):
         kk = r.kk[...]
         return state_block(r.cols[...], feature_pair(kk * shifted(kk, block)))
 
-    def key_tail():
-        ks = split(r.kk[...])
-        norm = dot3([k[:, :E] for k in ks], ks, TN)
-        return jnp.where(low, key_block(LAST), norm)
-
-    fill(at, earlier, key_block, key_tail)
+    for h in range(4):
+        if h == 3:
+            norms.relay()
+        fill(at, earlier[h], h, key_block)
 
     def query_feature(block, carry):
         qq = r.qq[...]
@@ -330,10 +378,20 @@
     r.dots[...] = dot3([v[:, :E] for v in qs], [v[:, :E] for v in ks], NT)
     weights = jnp.where(causal, r.dots[...] * r.dots[...] * (1.0 / E), 0.0)
     r.wgh[...], r.wgl[...] = split(weights)
-    r.numer[...] = dot3((r.wgh[...], r.wgl[...]), vs, NN)
-    r.denom[...] = jnp.broadcast_to(1.0 + jnp.sum(weights, axis=1, keepdims=True), (T, L))
-    for chunk in earlier:
-        chunk.prefixes()
+    near = 1.0 + jnp.sum(weights, axis=1, keepdims=True)
+
+    r.normed[...] = dot3([v[:, :E] for v in qs], norms.result(), NN)
+    denom = near + jnp.sum(r.normed[...] * r.qq[...], axis=1, keepdims=True) * (0.5 / E)
+    r.inverse[...] = jnp.broadcast_to(1.0 / denom, (T, L))
+    r.gn[...] = doubled(r.gg[...]) * r.inverse[...]
+    r.cols[...] = columns_of(r.gn[...])
+
+    def query_block(block):
+        return state_block(r.cols[...], r.feats[block])
+
+    for h in range(4):
+        earlier[h].prefixes()
+        fill(at, later[h], h, query_block)
 
     def transposed(b, carry):
         for to, value in ((r.xth, r.xh[b]), (r.xtl, r.xl[b])):
@@ -344,39 +402,31 @@
         return carry
 
     lax.fori_loop(0, NX, transposed, 0)
-    for chunk in earlier:
-        chunk.spread()
+    for h in range(4):
+        earlier[h].spread()
+        later[h].totals()
+
+    gs = split(r.gn[...])
+    r.numer[...] = dot3((r.wgh[...], r.wgl[...]), vs, NN)
+    r.dv[...] = dot3((r.wgh[...], r.wgl[...]), gs, TN)
+    r.scores[...] = dot3([v[:, :E] for v in gs], [v[:, :E] for v in vs], NT)
+    r.rows[...] = rows_of(r.gn[...])
 
     def forward(block, parts, total):
         return total + apply_state(r.feats[block], parts)
 
     total = jnp.zeros((T, L), F32)
-    for h, chunk in enumerate(earlier):
-        total = over_blocks(at, chunk, h, forward, total, True)
-    tail = tail_of(earlier)
-    total = total + apply_state(r.feats[LAST], tail)
-    qs = split(r.qq[...])
-    normed = jnp.where(low, 0.0, dot3([v[:, :E] for v in qs], tail, NN))
-    denom = r.denom[...] + jnp.sum(normed * r.qq[...], axis=1, keepdims=True) * (1.0 / E)
-    inverse = 1.0 / denom
-    grad_numer = doubled(r.gg[...]) * inverse
-    grad_denom = -0.5 * jnp.sum(grad_numer * (r.numer[...] + folded(total)), axis=1, keepdims=True) * inverse
-    r.gn[...] = grad_numer
-    r.gd[...] = grad_denom
-
-    r.cols[...] = columns_of(grad_numer)
-
-    def query_block(block):
-        return state_block(r.cols[...], r.feats[block])
-
-    def query_tail():
-        qq = r.qq[...]
-        norm = dot3(split((qq * r.gd[...])[:, :E]), split(qq), TN) * (1.0 / E)
-        return jnp.where(low, query_block(LAST), norm)
-
-    fill(at, later, query_block, query_tail)
-
-    r.rows[...] = rows_of(r.gn[...])
+    for h in range(4):
+        total = over_blocks(at, earlier[h], h, forward, total, True)
+        if h >= 2:
+            later[h - 2].prefixes()
+    total = total + apply_state(r.feats[LAST], tail_of(earlier))
+    outputs = r.numer[...] + folded(total)
+    r.gd[...] = jnp.sum(r.gn[...] * outputs, axis=1, keepdims=True) * r.inverse[...] * -0.5
+    qq = r.qq[...]
+    adjoint_norms.start(dot3(split((qq * r.gd[...])[:, :E]), split(qq), TN) * (1.0 / E))
+    later[2].prefixes()
+    later[3].prefixes()
 
     def backward(block, parts, carry):
         one, two = carry
@@ -384,22 +434,25 @@
         grad = apply_rows(r.rows[...], parts) * query_scale(block)
         return one + grad * shifted(qq, block), two + unshifted(grad * qq, block)
 
-    r.one[...] = normed * r.gd[...] * (2.0 / E)
+    r.one[...] = r.normed[...] * r.gd[...] * (1.0 / E)
     r.two[...] = jnp.zeros((T, L), F32)
-    for h, chunk in enumerate(later):
-        chunk.totals()
+    for h in range(4):
         carry = (r.one[...], r.two[...])
         if h == 0:
             carry = backward(LAST, tail_of(earlier), carry)
         r.one[...], r.two[...] = over_blocks(at, earlier[h], h, backward, carry, False)
-    qs, ks, vs, gs = [split(ref[...]) for ref in (r.qq, r.kk, r.vv, r.gn)]
-    grad_scores = dot3([v[:, :E] for v in gs], [v[:, :E] for v in vs], NT) + r.gd[:, :1]
-    r.gdh[...], r.gdl[...] = split(jnp.where(causal, grad_scores, 0.0) * r.dots[...] * (2.0 / E))
+        if h == 2:
+            adjoint_norms.relay()
+    qs, ks = [split(ref[...]) for ref in (r.qq, r.kk)]
+    grad_scores = jnp.where(causal, r.scores[...] + r.gd[:, :1], 0.0)
+    r.gdh[...], r.gdl[...] = split(grad_scores * r.dots[...] * (2.0 / E))
     r.dq[...] = folded(r.one[...] + r.two[...]) + dot3((r.gdh[...], r.gdl[...]), ks, NN)
     give_q = remote(r.dq, r.dqo, r.cs.at[2], r.cr.at[2], sibling)
     give_q.start()
-    later[0].prefixes()
-    later[1].prefixes()
+    for chunk in later:
+        chunk.spread()
+    r.dk[...] = dot3((r.gdh[...], r.gdl[...]), qs, TN)
+    r.rows[...] = rows_of(r.vv[...])
     give_q.wait_recv()
     own_lanes = low == (c == 0)
     r.gh[0], r.gl[0] = split(jnp.where(own_lanes, r.dq[...], r.dqo[...]))
@@ -408,26 +461,13 @@
         grad = dot3((r.xth[rows], r.xtl[rows]), (r.gh[0], r.gl[0]), NN)
         for i in range(16):
             r.dwq[i % NY, 4 * h + i // NY] = grad[i * 16 : (i + 1) * 16]
-    q_y = [None] + [
-        remote(r.dwq.at[lax.rem(y + d, NY)], r.qry.at[d], r.qs1.at[d], r.qr1.at[d], at.py[d]) for d in range(1, NY)
+    q_y = [
+        remote(r.dwq.at[lax.rem(y + d, NY)], r.qry.at[d], r.qs.at[0], r.qr.at[0], at.py[d]) for d in (2, 1, 3)
     ]
-    for d in (2, 1, 3):
-        q_y[d].start()
-    later[2].prefixes()
-    later[3].prefixes()
-    r.dk[...] = dot3((r.gdh[...], r.gdl[...]), qs, TN)
-    r.dv[...] = dot3((r.wgh[...], r.wgl[...]), gs, TN)
-    r.rows[...] = rows_of(r.vv[...])
-    for chunk in later:
-        chunk.spread()
-    for d in (1, 3, 2):
-        q_y[d].wait_recv()
-    r.qty[...] = r.dwq[y] + r.qry[1] + r.qry[2] + r.qry[3]
-    q_z = [None] + [
-        remote(r.qty.at[lax.rem(z + d, NZ)], r.qrz.at[d], r.qs2.at[d], r.qr2.at[d], at.pz[d]) for d in range(1, NZ)
-    ]
-    for d in (4, 3, 5, 2, 6, 1, 7):
-        q_z[d].start()
+    for copy in q_y:
+        copy.start()
+    all_q_y = settle(r.qry.at[pl.ds(1, NY - 1)], r.qs.at[0], r.qr.at[0], at.py[1])
+    all_q_z = settle(r.qrz.at[pl.ds(1, NZ - 1)], r.qs.at[1], r.qr.at[1], at.pz[1])
 
     def keys(block, parts, carry, mask=None):
         total, one, two = carry
@@ -441,14 +481,18 @@
 
     zero = jnp.zeros((T, L), F32)
     carry = (zero, zero, zero)
-    for h, chunk in enumerate(later):
-        carry = over_blocks(at, chunk, h, keys, carry, True)
-    tail = tail_of(later)
-    total, one, two = keys(LAST, tail, carry, low)
+    for h in range(4):
+        carry = over_blocks(at, later[h], h, keys, carry, True)
+        if h == 2:
+            all_q_y.wait_recv()
+            r.qty[...] = r.dwq[y] + r.qry[1] + r.qry[2] + r.qry[3]
+            for d in (4, 3, 5, 2, 6, 1, 7):
+                remote(r.qty.at[lax.rem(z + d, NZ)], r.qrz.at[d], r.qs.at[1], r.qr.at[1], at.pz[d]).start()
+    total, one, two = keys(LAST, tail_of(later), carry, low)
     ks = split(r.kk[...])
-    normed = jnp.where(low, 0.0, dot3([v[:, :E] for v in ks], tail, NN))
+    normed = dot3([v[:, :E] for v in ks], adjoint_norms.result(), NN)
     dv = r.dv[...] + folded(total)
-    dk = r.dk[...] + folded(one + two + 2.0 * normed)
+    dk = r.dk[...] + folded(one + two) + 2.0 * normed
     r.kv[...] = jnp.where(low, dk, dv)
     give_kv = remote(r.kv, r.kvo, r.cs.at[3], r.cr.at[3], sibling)
     give_kv.start()
@@ -465,17 +509,12 @@
         grad = dot3((r.xth[rows], r.xtl[rows]), kv, NN)
         for i in range(16):
             r.dw[h, i % NY, i // NY] = grad[i * 16 : (i + 1) * 16]
-        first.append(
-            [None]
-            + [
-                remote(r.dw.at[h, lax.rem(y + d, NY)], r.wry.at[h, d], r.ws1.at[h, d], r.wr1.at[h, d], at.py[d])
-                for d in range(1, NY)
-            ]
-        )
         for d in (2, 1, 3):
-            first[h][d].start()
-
-    out_x = [None] * NX
+            remote(
+                r.dw.at[h, lax.rem(y + d, NY)], r.wry.at[h, d], r.ws.at[h], r.wr.at[h], at.py[d]
+            ).start()
+        first.append(settle(r.wry.at[h, pl.ds(1, NY - 1)], r.ws.at[h], r.wr.at[h], at.py[1]))
+
     for d in (2, 1, 3, 0):
         rows = pl.ds(pl.multiple_of(lax.rem(x + d, NX) * 256, 256), 256)
         part = jnp.zeros((128, 256), F32)
@@ -483,45 +522,38 @@
             part = part + dot3((r.gh[i, mine], r.gl[i, mine]), (r.wh[i, rows], r.wl[i, rows]), NT)
         r.sx[d] = part
         if d:
-            out_x[d] = remote(r.sx.at[d], r.rx.at[d], r.os.at[d], r.or_.at[d], at.px[d])
-            out_x[d].start()
+            remote(r.sx.at[d], r.rx.at[d], r.os.at[0], r.os.at[1], at.px[d]).start()
+    all_x = settle(r.rx.at[pl.ds(1, NX - 1)], r.os.at[0], r.os.at[1], at.px[1])
 
     for h in range(2):
-        for d in (1, 3, 2):
-            first[h][d].wait_recv()
+        first[h].wait_recv()
         r.wty[h] = r.dw[h, y] + r.wry[h, 1] + r.wry[h, 2] + r.wry[h, 3]
         for j in (0, 3, 1, 2):
             target = 4 * h + j
             d = lax.rem(target - z + NZ, NZ)
-            copy = remote(r.wty.at[h, j], r.wrz.at[d], r.ws2.at[d], r.wr2.at[d], device(x, y, target, c))
+            copy = remote(r.wty.at[h, j], r.wrz.at[d], r.ws.at[2], r.wr.at[2], device(x, y, target, c))
             pl.when(target != z)(copy.start)
-    for d in (1, 3, 2):
-        out_x[d].wait_recv()
+    all_x.wait_recv()
     r.gx[...] = r.sx[0] + r.rx[1] + r.rx[2] + r.rx[3]
+    all_q_z.wait_recv()
     total = r.qty[z]
     for d in range(1, NZ):
-        q_z[d].wait_recv()
         total = total + r.qrz[d]
     r.gw[0] = total
+    for copy in [own, grads, give_q, give_kv, all_q_y, all_q_z, all_x] + first:
+        copy.wait_send()
+    settle(r.xg.at[pl.ds(0, 3), pl.ds(0, 128)], r.xs, r.xr.at[0, 0], at.px[1]).wait_send()
+    settle(r.xg.at[pl.ds(0, 3), pl.ds(0, 128)], r.fs, r.fr.at[0, 0], sibling).wait_send()
+    for group in earlier + later + [norms, adjoint_norms]:
+        group.close()
+    all_z = settle(r.wrz.at[pl.ds(1, NZ - 1)], r.ws.at[2], r.wr.at[2], at.pz[1])
+    all_z.wait_recv()
     total = r.wty[lax.div(z, 4), lax.rem(z, 4)]
-    second = [
-        remote(
-            r.wty.at[lax.div(lax.rem(z + d, NZ), 4), lax.rem(z + d, 4)], r.wrz.at[d], r.ws2.at[d], r.wr2.at[d], at.pz[d]
-        )
-        for d in range(1, NZ)
-    ]
-    for d in (1, 7, 2, 6, 3, 5, 4):
-        second[d - 1].wait_recv()
+    for d in range(1, NZ):
         total = total + r.wrz[d]
     r.gw[1] = total[:, :L]
     r.gw[2] = total[:, L:]
-    sent = [own, grads, give_q, give_kv] + second
-    for group in over_x + forwards + first + [out_x, q_y, q_z]:
-        sent += group[1:]
-    for copy in sent:
-        copy.wait_send()
-    for chunk in earlier + later:
-        chunk.close()
+    all_z.wait_send()
 
 
 def fused(inputs, weights, out_grads):
@@ -548,7 +580,9 @@
         wgh=vm(T, T, dtype=BF16),
         wgl=vm(T, T, dtype=BF16),
         numer=vm(T, L),
-        denom=vm(T, L),
+        inverse=vm(T, L),
+        normed=vm(T, L),
+        scores=vm(T, T),
         gn=vm(T, L),
         gd=vm(T, L),
         one=vm(T, L),
@@ -579,22 +613,17 @@
     )
     sems = dict(
         wsem=dma,
-        xs=dma((2, NX)),
+        xs=dma,
         xr=dma((2, NX)),
-        fs=dma((2, NX)),
+        fs=dma,
         fr=dma((2, NX)),
         cs=dma((4,)),
         cr=dma((4,)),
-        qs1=dma((NY,)),
-        qr1=dma((NY,)),
-        qs2=dma((NZ,)),
-        qr2=dma((NZ,)),
-        ws1=dma((2, NY)),
-        wr1=dma((2, NY)),
-        ws2=dma((NZ,)),
-        wr2=dma((NZ,)),
-        os=dma((NX,)),
-        or_=dma((NX,)),
+        qs=dma((2,)),
+        qr=dma((2,)),
+        ws=dma((3,)),
+        wr=dma((3,)),
+        os=dma((2,)),
     )
     bufs = [
         [
@@ -613,15 +642,19 @@
         ]
         for _ in range(2)
     ]
-    scan_sems = [dma((2, len(CHUNKS), n)) for n in (NY, NY, NZ, NZ, NZ, NZ, NY, NY)]
-    flat = list(scratch.values()) + list(sems.values()) + [b for s in bufs for h in s for b in h] + scan_sems
+    small = [vm(*shape, 32, L) for _ in range(2) for shape in ((), (NY,), (), (NZ,))]
+    scan_sems = [dma((2, len(CHUNKS), 4)), dma((2, len(CHUNKS), 4)), dma((2, 2)), dma((2, 2))]
+    flat = list(scratch.values()) + list(sems.values()) + [b for s in bufs for h in s for b in h] + small + scan_sems
     names = ["x_in", "w_in", "g_in", "gx", "gw"] + list(scratch) + list(sems)
 
     def kernel(*refs):
         named, rest = refs[: len(names)], refs[len(names) :]
         count = len(CHUNKS)
         held = [[[rest[(s * count + h) * 9 + i] for h in range(count)] for s in range(2)] for i in range(9)]
-        fused_kernel(names + ["bufs", "sems"], *named, held, rest[18 * count :])
+        rest = rest[18 * count :]
+        fused_kernel(
+            names + ["bufs", "small", "sems", "small_sems"], *named, held, (rest[:4], rest[4:8]), rest[8:10], rest[10:]
+        )
 
     return pl.pallas_call(
         kernel,

time: 86.8 us -> 79.2 us (0.912)
  Pallas kernels: 86 us -> 78.4 us
    pallas_call x1, Pallas kernels: 84.4 us -> 76.9 us  [fused(): pl.pallas_call(kernel, out_shape=(jax.ShapeDtypeStruct((128, 256), F32),...]
where the time goes in v2:
time: 79.2 us; the launch traced here: 79.1 us
  Pallas kernels  78.4 us (99%)
    pallas_call x1, Pallas kernels, fused(): pl.pallas_call(kernel, out_shape=(jax.ShapeDtypeStruct((128, 256), F32),...  76.9 us

profile of v2, /device:TPU:1, one launch (start us, length us, event | category | flops | bytes accessed | tf_op | source)
XLA Modules:
  0.0 79.1 jit_solution(6548261287620325266)
XLA Ops:
  0.6 76.9 %fused.1 = (f32[128,256]{1,0:T(8,128)}, f32[3,16,128]{2,1,0:T(8,128)}) custom-call(f32[128,256]{1,0:T(8,128)} %refs_0_.1, f32[3,1024,128]{2,1,0:T(8,128)} %bitcast.2, f32[128,128]{1,0:T(8,128)} %refs_2_.1), custom_call_target="tpu_custom_call" | custom-call | tf_op jit(solution)/shard_map/fused/pallas_call | solution.py:659
  77.5 1.6 %finish.1 = (f32[128,256]{1,0:T(8,128)}, f32[3,16,128]{2,1,0:T(8,128)}) custom-call(f32[128,256]{1,0:T(8,128)} %get-tuple-element.6.gx, f32[3,16,128]{2,1,0:T(8,128)} %get-tuple-element.7.gw), custom_call_target="tpu_custom_call" | custom-call | tf_op jit(solution)/shard_map/finish/pallas_call | solution.py:677

commit v3 on v2

--- a/solution.py
+++ b/solution.py
@@ -359,7 +359,7 @@
         return state_block(r.cols[...], feature_pair(kk * shifted(kk, block)))
 
     for h in range(4):
-        if h == 3:
+        if h == 2:
             norms.relay()
         fill(at, earlier[h], h, key_block)
 
@@ -390,8 +390,9 @@
         return state_block(r.cols[...], r.feats[block])
 
     for h in range(4):
-        earlier[h].prefixes()
         fill(at, later[h], h, query_block)
+    for chunk in earlier:
+        chunk.prefixes()
 
     def transposed(b, carry):
         for to, value in ((r.xth, r.xh[b]), (r.xtl, r.xl[b])):
@@ -415,12 +416,27 @@
     def forward(block, parts, total):
         return total + apply_state(r.feats[block], parts)
 
-    total = jnp.zeros((T, L), F32)
+    def backward(block, parts, carry):
+        one, two = carry
+        qq = r.qq[...]
+        grad = apply_rows(r.rows[...], parts) * query_scale(block)
+        return one + grad * shifted(qq, block), two + unshifted(grad * qq, block)
+
+    r.one[...] = jnp.zeros((T, L), F32)
+    r.two[...] = jnp.zeros((T, L), F32)
+
+    def query_gradient(h):
+        carry = (r.one[...], r.two[...])
+        r.one[...], r.two[...] = over_blocks(at, earlier[h], h, backward, carry, False)
+
+    r.total[...] = jnp.zeros((T, L), F32)
     for h in range(4):
-        total = over_blocks(at, earlier[h], h, forward, total, True)
-        if h >= 2:
-            later[h - 2].prefixes()
-    total = total + apply_state(r.feats[LAST], tail_of(earlier))
+        r.total[...] = over_blocks(at, earlier[h], h, forward, r.total[...], True)
+        if h < 3:
+            query_gradient(h)
+        if h in (1, 2):
+            later[h - 1].prefixes()
+    total = r.total[...] + apply_state(r.feats[LAST], tail_of(earlier))
     outputs = r.numer[...] + folded(total)
     r.gd[...] = jnp.sum(r.gn[...] * outputs, axis=1, keepdims=True) * r.inverse[...] * -0.5
     qq = r.qq[...]
@@ -428,27 +444,16 @@
     later[2].prefixes()
     later[3].prefixes()
 
-    def backward(block, parts, carry):
-        one, two = carry
-        qq = r.qq[...]
-        grad = apply_rows(r.rows[...], parts) * query_scale(block)
-        return one + grad * shifted(qq, block), two + unshifted(grad * qq, block)
-
-    r.one[...] = r.normed[...] * r.gd[...] * (1.0 / E)
-    r.two[...] = jnp.zeros((T, L), F32)
-    for h in range(4):
-        carry = (r.one[...], r.two[...])
-        if h == 0:
-            carry = backward(LAST, tail_of(earlier), carry)
-        r.one[...], r.two[...] = over_blocks(at, earlier[h], h, backward, carry, False)
-        if h == 2:
-            adjoint_norms.relay()
+    query_gradient(3)
+    carry = backward(LAST, tail_of(earlier), (r.one[...] + r.normed[...] * r.gd[...] * (1.0 / E), r.two[...]))
+    r.one[...], r.two[...] = carry
     qs, ks = [split(ref[...]) for ref in (r.qq, r.kk)]
     grad_scores = jnp.where(causal, r.scores[...] + r.gd[:, :1], 0.0)
     r.gdh[...], r.gdl[...] = split(grad_scores * r.dots[...] * (2.0 / E))
     r.dq[...] = folded(r.one[...] + r.two[...]) + dot3((r.gdh[...], r.gdl[...]), ks, NN)
     give_q = remote(r.dq, r.dqo, r.cs.at[2], r.cr.at[2], sibling)
     give_q.start()
+    adjoint_norms.relay()
     for chunk in later:
         chunk.spread()
     r.dk[...] = dot3((r.gdh[...], r.gdl[...]), qs, TN)
@@ -464,8 +469,6 @@
     q_y = [
         remote(r.dwq.at[lax.rem(y + d, NY)], r.qry.at[d], r.qs.at[0], r.qr.at[0], at.py[d]) for d in (2, 1, 3)
     ]
-    for copy in q_y:
-        copy.start()
     all_q_y = settle(r.qry.at[pl.ds(1, NY - 1)], r.qs.at[0], r.qr.at[0], at.py[1])
     all_q_z = settle(r.qrz.at[pl.ds(1, NZ - 1)], r.qs.at[1], r.qr.at[1], at.pz[1])
 
@@ -482,12 +485,11 @@
     zero = jnp.zeros((T, L), F32)
     carry = (zero, zero, zero)
     for h in range(4):
-        carry = over_blocks(at, later[h], h, keys, carry, True)
-        if h == 2:
-            all_q_y.wait_recv()
-            r.qty[...] = r.dwq[y] + r.qry[1] + r.qry[2] + r.qry[3]
-            for d in (4, 3, 5, 2, 6, 1, 7):
-                remote(r.qty.at[lax.rem(z + d, NZ)], r.qrz.at[d], r.qs.at[1], r.qr.at[1], at.pz[d]).start()
+        if h == 3:
+            later[3].all_of(3).wait_recv()
+            for copy in q_y:
+                copy.start()
+        carry = over_blocks(at, later[h], h, keys, carry, h < 3)
     total, one, two = keys(LAST, tail_of(later), carry, low)
     ks = split(r.kk[...])
     normed = dot3([v[:, :E] for v in ks], adjoint_norms.result(), NN)
@@ -514,6 +516,11 @@
                 r.dw.at[h, lax.rem(y + d, NY)], r.wry.at[h, d], r.ws.at[h], r.wr.at[h], at.py[d]
             ).start()
         first.append(settle(r.wry.at[h, pl.ds(1, NY - 1)], r.ws.at[h], r.wr.at[h], at.py[1]))
+
+    all_q_y.wait_recv()
+    r.qty[...] = r.dwq[y] + r.qry[1] + r.qry[2] + r.qry[3]
+    for d in (4, 3, 5, 2, 6, 1, 7):
+        remote(r.qty.at[lax.rem(z + d, NZ)], r.qrz.at[d], r.qs.at[1], r.qr.at[1], at.pz[d]).start()
 
     for d in (2, 1, 3, 0):
         rows = pl.ds(pl.multiple_of(lax.rem(x + d, NX) * 256, 256), 256)
@@ -582,6 +589,7 @@
         numer=vm(T, L),
         inverse=vm(T, L),
         normed=vm(T, L),
+        total=vm(T, L),
         scores=vm(T, T),
         gn=vm(T, L),
         gd=vm(T, L),

time: 79.2 us -> 75.3 us (0.951)
  Pallas kernels: 78.4 us -> 74.5 us
    pallas_call x1, Pallas kernels: 76.9 us -> 72.9 us  [fused(): pl.pallas_call(kernel, out_shape=(jax.ShapeDtypeStruct((128, 256), F32),...]
where the time goes in v3:
time: 75.3 us; the launch traced here: 75.1 us
  Pallas kernels  74.5 us (99%)
    pallas_call x1, Pallas kernels, fused(): pl.pallas_call(kernel, out_shape=(jax.ShapeDtypeStruct((128, 256), F32),...  72.9 us
    pallas_call x1, Pallas kernels, per_device(): pl.pallas_call(finish_kernel, out_shape=(jax.ShapeDtypeStruct((128, 256),...  1.57 us

profile of v3, /device:TPU:1, one launch (start us, length us, event | category | flops | bytes accessed | tf_op | source)
XLA Modules:
  0.0 75.1 jit_solution(11958889422921209761)
XLA Ops:
  0.6 72.9 %fused.1 = (f32[128,256]{1,0:T(8,128)}, f32[3,16,128]{2,1,0:T(8,128)}) custom-call(f32[128,256]{1,0:T(8,128)} %refs_0_.1, f32[3,1024,128]{2,1,0:T(8,128)} %bitcast.2, f32[128,128]{1,0:T(8,128)} %refs_2_.1), custom_call_target="tpu_custom_call" | custom-call | tf_op jit(solution)/shard_map/fused/pallas_call | solution.py:667
  73.5 1.6 %finish.1 = (f32[128,256]{1,0:T(8,128)}, f32[3,16,128]{2,1,0:T(8,128)}) custom-call(f32[128,256]{1,0:T(8,128)} %get-tuple-element.6.gx, f32[3,16,128]{2,1,0:T(8,128)} %get-tuple-element.7.gw), custom_call_target="tpu_custom_call" | custom-call | tf_op jit(solution)/shard_map/finish/pallas_call | solution.py:685

commit v4 on v3

--- a/solution.py
+++ b/solution.py
@@ -282,15 +282,16 @@
     at.pz = [None] + [device(x, y, lax.rem(z + d, NZ), c) for d in range(1, NZ)]
     low = lower()
 
-    load = pltpu.make_async_copy(r.w_in, r.w, r.wsem)
-    load.start()
     barrier = pltpu.get_barrier_semaphore()
     peers = [sibling] + at.px[1:] + at.py[1:] + at.pz[1:]
     for peer in peers:
         pl.semaphore_signal(barrier, inc=1, device_id=peer, device_id_type=MESH)
     mine = pl.ds(pl.multiple_of(c * 128, 128), 128)
-    r.xg[x, mine] = r.x_in[...]
-    r.gg[mine] = r.g_in[...]
+    load_x = pltpu.make_async_copy(r.x_in, r.xg.at[x, mine], r.wsem.at[1])
+    load_g = pltpu.make_async_copy(r.g_in, r.gg.at[mine], r.wsem.at[2])
+    load = pltpu.make_async_copy(r.w_in, r.w, r.wsem.at[0])
+    for copy in (load_x, load_g, load):
+        copy.start()
     load.wait()
 
     def split_weights(b, carry):
@@ -300,6 +301,8 @@
         return carry
 
     lax.fori_loop(0, NX, split_weights, 0)
+    load_x.wait()
+    load_g.wait()
     pl.semaphore_wait(barrier, len(peers))
 
     over_x = [[None] * NX, [None] * NX]
@@ -308,12 +311,12 @@
     for k in range(2):
         for d in (2, 1, 3):
             over_x[k][d] = remote(
-                r.x_in.at[pl.ds(64 * k, 64)], r.xg.at[x, halves[k]], r.xs, r.xr.at[k, d], at.px[d]
+                r.xg.at[x, halves[k]], r.xg.at[x, halves[k]], r.xs, r.xr.at[k, d], at.px[d]
             )
             over_x[k][d].start()
-    own = remote(r.x_in, r.xg.at[x, mine], r.cs.at[0], r.cr.at[0], sibling)
+    own = remote(r.xg.at[x, mine], r.xg.at[x, mine], r.cs.at[0], r.cr.at[0], sibling)
     own.start()
-    grads = remote(r.g_in, r.gg.at[mine], r.cs.at[1], r.cr.at[1], sibling)
+    grads = remote(r.gg.at[mine], r.gg.at[mine], r.cs.at[1], r.cr.at[1], sibling)
     grads.start()
 
     def project(b, sums):
@@ -620,7 +623,7 @@
         rx=vm(NX, 128, 256),
     )
     sems = dict(
-        wsem=dma,
+        wsem=dma((3,)),
         xs=dma,
         xr=dma((2, NX)),
         fs=dma,
@@ -667,7 +670,7 @@
     return pl.pallas_call(
         kernel,
         out_shape=(jax.ShapeDtypeStruct((128, 256), F32), jax.ShapeDtypeStruct((3, 16, L), F32)),
-        in_specs=[VMEM, pl.BlockSpec(memory_space=pl.ANY), VMEM],
+        in_specs=[pl.BlockSpec(memory_space=pl.ANY)] * 3,
         out_specs=(VMEM, VMEM),
         scratch_shapes=flat,
         compiler_params=pltpu.CompilerParams(collective_id=0, has_side_effects=True, vmem_limit_bytes=LIMIT),

time: 75.3 us -> 74.1 us (0.984)
  Pallas kernels: 74.5 us -> 73.4 us
    pallas_call x1, Pallas kernels: 72.9 us -> 71.8 us  [fused(): pl.pallas_call(kernel, out_shape=(jax.ShapeDtypeStruct((128, 256), F32),...]
where the time goes in v4:
time: 74.1 us; the launch traced here: 74 us
  Pallas kernels  73.4 us (99%)
    pallas_call x1, Pallas kernels, fused(): pl.pallas_call(kernel, out_shape=(jax.ShapeDtypeStruct((128, 256), F32),...  71.8 us
    pallas_call x1, Pallas kernels, per_device(): pl.pallas_call(finish_kernel, out_shape=(jax.ShapeDtypeStruct((128, 256),...  1.57 us

profile of v4, /device:TPU:1, one launch (start us, length us, event | category | flops | bytes accessed | tf_op | source)
XLA Modules:
  0.0 74.0 jit_solution(17245823441699034433)
XLA Ops:
  0.6 71.8 %fused.1 = (f32[128,256]{1,0:T(8,128)}, f32[3,16,128]{2,1,0:T(8,128)}) custom-call(f32[128,256]{1,0:T(8,128)} %refs_0_.1, f32[3,1024,128]{2,1,0:T(8,128)} %bitcast.2, f32[128,128]{1,0:T(8,128)} %refs_2_.1), custom_call_target="tpu_custom_call" | custom-call | tf_op jit(solution)/shard_map/fused/pallas_call | solution.py:670
  72.4 1.6 %finish.1 = (f32[128,256]{1,0:T(8,128)}, f32[3,16,128]{2,1,0:T(8,128)}) custom-call(f32[128,256]{1,0:T(8,128)} %get-tuple-element.6.gx, f32[3,16,128]{2,1,0:T(8,128)} %get-tuple-element.7.gw), custom_call_target="tpu_custom_call" | custom-call | tf_op jit(solution)/shard_map/finish/pallas_call | solution.py:688

commit v5 on v4

--- a/solution.py
+++ b/solution.py
@@ -309,7 +309,7 @@
     forwards = [[None] * NX, [None] * NX]
     halves = [pl.ds(pl.multiple_of(c * 128 + 64 * k, 64), 64) for k in range(2)]
     for k in range(2):
-        for d in (2, 1, 3):
+        for d in (1, 3, 2):
             over_x[k][d] = remote(
                 r.xg.at[x, halves[k]], r.xg.at[x, halves[k]], r.xs, r.xr.at[k, d], at.px[d]
             )
@@ -495,24 +495,26 @@
         carry = over_blocks(at, later[h], h, keys, carry, h < 3)
     total, one, two = keys(LAST, tail_of(later), carry, low)
     ks = split(r.kk[...])
+    dv = r.dv[...] + folded(total)
+    r.kv[0] = dv
+    give_v = remote(r.kv.at[0], r.kvo.at[0], r.cs.at[3], r.cr.at[3], sibling)
+    give_v.start()
     normed = dot3([v[:, :E] for v in ks], adjoint_norms.result(), NN)
-    dv = r.dv[...] + folded(total)
     dk = r.dk[...] + folded(one + two) + 2.0 * normed
-    r.kv[...] = jnp.where(low, dk, dv)
-    give_kv = remote(r.kv, r.kvo, r.cs.at[3], r.cr.at[3], sibling)
-    give_kv.start()
-    give_kv.wait_recv()
-    other = r.kvo[...]
-    turned = roll(other, E)
-    r.gh[1], r.gl[1] = split(jnp.where(own_lanes, dk, jnp.where(c == 0, turned, other)))
-    r.gh[2], r.gl[2] = split(jnp.where(own_lanes, dv, jnp.where(c == 0, other, turned)))
+    r.kv[1] = dk
+    give_k = remote(r.kv.at[1], r.kvo.at[1], r.cs.at[4], r.cr.at[4], sibling)
+    give_k.start()
+    give_v.wait_recv()
+    r.gh[2], r.gl[2] = split(jnp.where(own_lanes, dv, r.kvo[0]))
+    give_k.wait_recv()
+    r.gh[1], r.gl[1] = split(jnp.where(own_lanes, dk, r.kvo[1]))
 
     kv = [jnp.concatenate([g[1], g[2]], axis=1) for g in (r.gh, r.gl)]
     first = []
-    for h in range(2):
-        rows = pl.ds(h * 256, 256)
+    for h in range(4):
+        rows = pl.ds(h * 128, 128)
         grad = dot3((r.xth[rows], r.xtl[rows]), kv, NN)
-        for i in range(16):
+        for i in range(8):
             r.dw[h, i % NY, i // NY] = grad[i * 16 : (i + 1) * 16]
         for d in (2, 1, 3):
             remote(
@@ -535,13 +537,13 @@
             remote(r.sx.at[d], r.rx.at[d], r.os.at[0], r.os.at[1], at.px[d]).start()
     all_x = settle(r.rx.at[pl.ds(1, NX - 1)], r.os.at[0], r.os.at[1], at.px[1])
 
-    for h in range(2):
+    for h in range(4):
         first[h].wait_recv()
         r.wty[h] = r.dw[h, y] + r.wry[h, 1] + r.wry[h, 2] + r.wry[h, 3]
-        for j in (0, 3, 1, 2):
-            target = 4 * h + j
+        for j in range(2):
+            target = 2 * h + j
             d = lax.rem(target - z + NZ, NZ)
-            copy = remote(r.wty.at[h, j], r.wrz.at[d], r.ws.at[2], r.wr.at[2], device(x, y, target, c))
+            copy = remote(r.wty.at[h, j], r.wrz.at[d], r.ws.at[4], r.wr.at[4], device(x, y, target, c))
             pl.when(target != z)(copy.start)
     all_x.wait_recv()
     r.gx[...] = r.sx[0] + r.rx[1] + r.rx[2] + r.rx[3]
@@ -550,15 +552,15 @@
     for d in range(1, NZ):
         total = total + r.qrz[d]
     r.gw[0] = total
-    for copy in [own, grads, give_q, give_kv, all_q_y, all_q_z, all_x] + first:
+    for copy in [own, grads, give_q, give_k, give_v, all_q_y, all_q_z, all_x] + first:
         copy.wait_send()
     settle(r.xg.at[pl.ds(0, 3), pl.ds(0, 128)], r.xs, r.xr.at[0, 0], at.px[1]).wait_send()
     settle(r.xg.at[pl.ds(0, 3), pl.ds(0, 128)], r.fs, r.fr.at[0, 0], sibling).wait_send()
     for group in earlier + later + [norms, adjoint_norms]:
         group.close()
-    all_z = settle(r.wrz.at[pl.ds(1, NZ - 1)], r.ws.at[2], r.wr.at[2], at.pz[1])
+    all_z = settle(r.wrz.at[pl.ds(1, NZ - 1)], r.ws.at[4], r.wr.at[4], at.pz[1])
     all_z.wait_recv()
-    total = r.wty[lax.div(z, 4), lax.rem(z, 4)]
+    total = r.wty[lax.div(z, 2), lax.rem(z, 2)]
     for d in range(1, NZ):
         total = total + r.wrz[d]
     r.gw[1] = total[:, :L]
@@ -604,8 +606,8 @@
         gdh=vm(T, T, dtype=BF16),
         gdl=vm(T, T, dtype=BF16),
         dqo=vm(T, L),
-        kv=vm(T, L),
-        kvo=vm(T, L),
+        kv=vm(2, T, L),
+        kvo=vm(2, T, L),
         gh=vm(3, T, L, dtype=BF16),
         gl=vm(3, T, L, dtype=BF16),
         turned=vm(256, T, dtype=BF16),
@@ -615,9 +617,9 @@
         qry=vm(NY, NZ, 16, L),
         qty=vm(NZ, 16, L),
         qrz=vm(NZ, 16, L),
-        dw=vm(2, NY, 4, 16, 2 * L),
-        wry=vm(2, NY, 4, 16, 2 * L),
-        wty=vm(2, 4, 16, 2 * L),
+        dw=vm(4, NY, 2, 16, 2 * L),
+        wry=vm(4, NY, 2, 16, 2 * L),
+        wty=vm(4, 2, 16, 2 * L),
         wrz=vm(NZ, 16, 2 * L),
         sx=vm(NX, 128, 256),
         rx=vm(NX, 128, 256),
@@ -628,12 +630,12 @@
         xr=dma((2, NX)),
         fs=dma,
         fr=dma((2, NX)),
-        cs=dma((4,)),
-        cr=dma((4,)),
+        cs=dma((5,)),
+        cr=dma((5,)),
         qs=dma((2,)),
         qr=dma((2,)),
-        ws=dma((3,)),
-        wr=dma((3,)),
+        ws=dma((5,)),
+        wr=dma((5,)),
         os=dma((2,)),
     )
     bufs = [

time: 74.1 us -> 72.8 us (0.982)
  Pallas kernels: 73.4 us -> 72 us
    pallas_call x1, Pallas kernels: 71.8 us -> 70.5 us  [fused(): pl.pallas_call(kernel, out_shape=(jax.ShapeDtypeStruct((128, 256), F32),...]
where the time goes in v5:
time: 72.8 us; the launch traced here: 72.7 us
  Pallas kernels  72 us (99%)
    pallas_call x1, Pallas kernels, fused(): pl.pallas_call(kernel, out_shape=(jax.ShapeDtypeStruct((128, 256), F32),...  70.5 us
    pallas_call x1, Pallas kernels, per_device(): pl.pallas_call(finish_kernel, out_shape=(jax.ShapeDtypeStruct((128, 256),...  1.57 us

profile of v5, /device:TPU:1, one launch (start us, length us, event | category | flops | bytes accessed | tf_op | source)
XLA Modules:
  0.0 72.7 jit_solution(6496387484588921741)
XLA Ops:
  0.6 70.5 %fused.1 = (f32[128,256]{1,0:T(8,128)}, f32[3,16,128]{2,1,0:T(8,128)}) custom-call(f32[128,256]{1,0:T(8,128)} %refs_0_.1, f32[3,1024,128]{2,1,0:T(8,128)} %bitcast.2, f32[128,128]{1,0:T(8,128)} %refs_2_.1), custom_call_target="tpu_custom_call" | custom-call | tf_op jit(solution)/shard_map/fused/pallas_call | solution.py:672
  71.1 1.6 %finish.1 = (f32[128,256]{1,0:T(8,128)}, f32[3,16,128]{2,1,0:T(8,128)}) custom-call(f32[128,256]{1,0:T(8,128)} %get-tuple-element.6.gx, f32[3,16,128]{2,1,0:T(8,128)} %get-tuple-element.7.gw), custom_call_target="tpu_custom_call" | custom-call | tf_op jit(solution)/shard_map/finish/pallas_call | solution.py:690

commit v6 on v5

--- a/solution.py
+++ b/solution.py
@@ -448,6 +448,8 @@
     later[3].prefixes()
 
     query_gradient(3)
+    later[0].spread()
+    later[1].spread()
     carry = backward(LAST, tail_of(earlier), (r.one[...] + r.normed[...] * r.gd[...] * (1.0 / E), r.two[...]))
     r.one[...], r.two[...] = carry
     qs, ks = [split(ref[...]) for ref in (r.qq, r.kk)]
@@ -457,7 +459,7 @@
     give_q = remote(r.dq, r.dqo, r.cs.at[2], r.cr.at[2], sibling)
     give_q.start()
     adjoint_norms.relay()
-    for chunk in later:
+    for chunk in later[2:]:
         chunk.spread()
     r.dk[...] = dot3((r.gdh[...], r.gdl[...]), qs, TN)
     r.rows[...] = rows_of(r.vv[...])

time: 72.8 us -> 71.6 us (0.984)
  Pallas kernels: 72 us -> 70.8 us
    pallas_call x1, Pallas kernels: 70.5 us -> 69.3 us  [fused(): pl.pallas_call(kernel, out_shape=(jax.ShapeDtypeStruct((128, 256), F32),...]
where the time goes in v6:
time: 71.6 us; the launch traced here: 71.5 us
  Pallas kernels  70.8 us (99%)
    pallas_call x1, Pallas kernels, fused(): pl.pallas_call(kernel, out_shape=(jax.ShapeDtypeStruct((128, 256), F32),...  69.3 us
    pallas_call x1, Pallas kernels, per_device(): pl.pallas_call(finish_kernel, out_shape=(jax.ShapeDtypeStruct((128, 256),...  1.57 us

profile of v6, /device:TPU:1, one launch (start us, length us, event | category | flops | bytes accessed | tf_op | source)
XLA Modules:
  0.0 71.5 jit_solution(8548308964883873342)
XLA Ops:
  0.6 69.3 %fused.1 = (f32[128,256]{1,0:T(8,128)}, f32[3,16,128]{2,1,0:T(8,128)}) custom-call(f32[128,256]{1,0:T(8,128)} %refs_0_.1, f32[3,1024,128]{2,1,0:T(8,128)} %bitcast.2, f32[128,128]{1,0:T(8,128)} %refs_2_.1), custom_call_target="tpu_custom_call" | custom-call | tf_op jit(solution)/shard_map/fused/pallas_call | solution.py:674
  69.9 1.6 %finish.1 = (f32[128,256]{1,0:T(8,128)}, f32[3,16,128]{2,1,0:T(8,128)}) custom-call(f32[128,256]{1,0:T(8,128)} %get-tuple-element.6.gx, f32[3,16,128]{2,1,0:T(8,128)} %get-tuple-element.7.gw), custom_call_target="tpu_custom_call" | custom-call | tf_op jit(solution)/shard_map/finish/pallas_call | solution.py:692
